TPU v7x, 512 devices: a whole 4x4x16 slice. The times are simulated.
512 devices in a mesh: rows: 128 (over z_lo, y, x, core), cols: 4 (over z_hi).
Axes of the slice: x: 4, y: 4, z: 16 (z_hi: 4, z_lo: 4; z = z_hi * 4 + z_lo), core: 2. Of those that a mesh axis runs over, the one named last changes fastest.
Arguments:
- solves: float32 [64, 524288], P('cols', 'rows'), may hold values from -6 to 6
- factor3: float32 [64, 524288], P('cols', 'rows')
- factor2: float32 [64, 524288], P('cols', 'rows')
- factor1: float32 [64, 524288], P('cols', 'rows')
- basis3: float32 [64, 524288], P(None, 'rows')
- basis2: float32 [64, 524288], P(None, 'rows')
- basis1: float32 [64, 524288], P(None, 'rows')
Outputs:
- solution: float32 [64, 524288], P('cols', 'rows')
All inputs are finite; a program needn't handle non-finite values.
Results may differ from a plain program's by a relative error of at most 0.000053.
Values sent between devices are 32-bit elements; how exact they have to be, the bound alone decides.
No kernel may reach another device: no remote copies, remote signals or barrier semaphores. Data moves between devices by JAX's collectives and lax.ppermute only.
A program may use at most 64 MiB of HBM per device.

v0:
```python
import jax
import jax.numpy as jnp
from jax import lax
from jax.sharding import PartitionSpec as P

RANK = 64
NRHS = 64


highest = lax.Precision.HIGHEST


def small_product(left_matrix, right_matrix):
    return jnp.matmul(left_matrix, right_matrix, precision=highest)


def solve_small(matrix, right_side):
    turned = jnp.swapaxes(matrix, -1, -2)
    lower_factor = jnp.linalg.cholesky(small_product(turned, matrix))
    return jax.scipy.linalg.cho_solve((lower_factor, True), small_product(turned, right_side))


def keep_part(values):
    return jnp.concatenate([values[..., :NRHS], values[..., NRHS + RANK :]], -1)


def combine(first_child, second_child):
    coupling_first = first_child[..., 0, :, NRHS : NRHS + RANK]
    coupling_second = second_child[..., 0, :, NRHS : NRHS + RANK]
    upper_side = keep_part(second_child[..., 0, :, :])
    lower_side = keep_part(first_child[..., 0, :, :])
    reduced = jnp.eye(RANK, dtype=jnp.float32) - small_product(coupling_first, coupling_second)
    lower_half = solve_small(reduced, lower_side - small_product(coupling_first, upper_side))
    upper_half = upper_side - small_product(coupling_second, lower_half)
    carried = keep_part(first_child[..., 1:, :, :]) - small_product(
        first_child[..., 1:, :, NRHS : NRHS + RANK], upper_half[..., None, :, :]
    )
    carried = (
        carried
        + keep_part(second_child[..., 1:, :, :])
        - small_product(second_child[..., 1:, :, NRHS : NRHS + RANK], lower_half[..., None, :, :])
    )
    return (carried, upper_half, lower_half)


def expand_rows(following, half_matrix):
    return jnp.concatenate(
        [following[:NRHS], -small_product(half_matrix, following), following[NRHS:]], 0
    )


def full_columns(gathered, col_count, column_local, rank_local):
    lead_shape = gathered.shape[:-1]
    shaped = gathered.reshape(lead_shape + (col_count, column_local + 3 * rank_local))
    offsets = [
        (0, column_local),
        (column_local, rank_local),
        (column_local + rank_local, rank_local),
        (column_local + 2 * rank_local, rank_local),
    ]
    pieces = [
        shaped[..., start_at : start_at + width_here].reshape(
            lead_shape + (col_count * width_here,)
        )
        for start_at, width_here in offsets
    ]
    return jnp.concatenate(pieces, -1)


def choose_half(upper_half, lower_half, position, parity):
    upper_pick = lax.dynamic_index_in_dim(upper_half, position, 0, keepdims=False)
    lower_pick = lax.dynamic_index_in_dim(lower_half, position, 0, keepdims=False)
    return jnp.where(parity == 0, upper_pick, lower_pick)


def whole_tree(node_sums, leaf_node):
    carried_two, upper_two, lower_two = combine(node_sums[0::2], node_sums[1::2])
    carried_one, upper_one, lower_one = combine(carried_two[0::2], carried_two[1::2])
    leftover, upper_root, lower_root = combine(carried_one[0:1], carried_one[1:2])
    level2_half = choose_half(upper_two, lower_two, leaf_node // 2, leaf_node % 2)
    level1_half = choose_half(upper_one, lower_one, leaf_node // 4, leaf_node // 2 % 2)
    root_half = choose_half(upper_root, lower_root, 0, leaf_node // 4 % 2)
    return (level2_half, level1_half, root_half)


def on_device(solves, factor3, factor2, factor1, basis3, basis2, basis1):
    col_count = lax.axis_size("cols")
    group_size = lax.axis_size("rows") // 8
    column_local = solves.shape[0]
    rank_local = factor3.shape[0]
    row_index = lax.axis_index("rows")
    col_index = lax.axis_index("cols")
    leaf_node = row_index // group_size
    stacked = jnp.concatenate([solves, factor3, factor2, factor1], 0)
    local_terms = jnp.stack(
        [
            lax.dot_general(
                basis_matrix,
                stacked,
                (((1,), (1,)), ((), ())),
                precision=highest,
                preferred_element_type=jnp.float32,
            )
            for basis_matrix in (basis3, basis2, basis1)
        ]
    )
    everyone = lax.all_gather(local_terms[None], "rows", axis=0, tiled=True)
    node_terms = everyone.reshape((8, group_size) + local_terms.shape).sum(1)
    node_sums = full_columns(
        lax.all_gather(node_terms, "cols", axis=3, tiled=True), col_count, column_local, rank_local
    )
    level2_half, level1_half, root_half = whole_tree(node_sums, leaf_node)
    coefficient = expand_rows(jnp.eye(NRHS, dtype=jnp.float32), root_half)
    coefficient = expand_rows(coefficient, level1_half)
    coefficient = expand_rows(coefficient, level2_half)[NRHS:]
    gathered = (
        lax.all_gather(factor3, "cols", axis=0, tiled=True),
        lax.all_gather(factor2, "cols", axis=0, tiled=True),
        lax.all_gather(factor1, "cols", axis=0, tiled=True),
    )
    own_columns = lax.dynamic_slice_in_dim(coefficient, col_index * column_local, column_local, 1)
    result = solves
    for level_slot in range(3):
        result = result + lax.dot_general(
            own_columns[level_slot * RANK : (level_slot + 1) * RANK],
            gathered[level_slot],
            (((0,), (0,)), ((), ())),
            precision=highest,
            preferred_element_type=jnp.float32,
        )
    return result


def solution(mesh):
    return jax.shard_map(
        on_device,
        mesh=mesh,
        in_specs=(
            P("cols", "rows"),
            P("cols", "rows"),
            P("cols", "rows"),
            P("cols", "rows"),
            P(None, "rows"),
            P(None, "rows"),
            P(None, "rows"),
        ),
        out_specs=P("cols", "rows"),
        check_vma=False,
    )
```

profile of v0, /device:TPU:1, one launch (start us, length us, event | category | flops | bytes accessed | tf_op | source)
XLA Modules:
  0.0 559.3 jit_solution(1909258218167243775)
XLA Ops:
  6.5 1.1 constant_dynamic-update-slice_fusion.3
  13.8 222.1 %all-gather.15.cloned.1.call-done = f32[384,64,64]{2,1,0:T(8,128)} async-done(((f32[3,64,64]{2,1,0:T(8,128)}), f32[384,64,64]{2,1,0:T(8,128)}) %all-gather.15.cloned.1.call-update) | async-done | bytes 6291472 | tf_op jit(solution)/shard_map/all_gather | solution.py:107
  235.9 6.2 %reduce_sum.9 = f32[8,3,64,64]{3,2,1,0:T(8,128)S(1)} reduce(f32[8,16,3,64,64]{4,3,2,1,0:T(8,128)} %bitcast.174, f32[]{:T(128)} %constant.228.clone.1), dimensions={1}, to_apply=%region_0.1 | reduce | flops 1474560 | bytes 6684676 | tf_op jit(solution)/shard_map/reduce_sum | solution.py:108
  242.1 1.2 copy.111
  245.4 125.3 %all-gather.7.cloned.1.call-done = f32[8,3,64,256]{2,0,1,3:T(8,128)} async-done(((f32[8,3,64,64]{2,0,1,3:T(8,128)}), f32[8,3,64,256]{2,0,1,3:T(8,128)}) %all-gather.7.cloned.1.call-update) | async-done | bytes 1572880 | tf_op jit(solution)/shard_map/all_gather | solution.py:110
  370.7 2.5 copy.112
  373.2 1.6 fusion.58
  374.7 1.4 copy.113
  376.1 2.3 copy.114
  378.4 1.1 copy.115
  379.6 1.2 copy.116
  380.8 2.0 pad_maximum_fusion
  388.1 24.2 %custom-call.33 = f32[4,64,64]{2,1,0:T(8,128)S(1)} custom-call(f32[4,64,64]{2,1,0:T(8,128)} %fusion.15), custom_call_target="Cholesky" | custom-call | tf_op jit(solution)/shard_map/jit(cholesky)/cholesky | solution.py:19
  412.5 20.3 %custom-call.34 = f32[4,1,64,64]{2,3,1,0:T(8,128)} custom-call(f32[4,1,64,64]{3,2,1,0:T(8,128)S(1)} %select_bitcast_fusion), custom_call_target="InvertDiagBlocksLowerTriangular" | custom-call | tf_op jit(solution)/shard_map/jit(_cho_solve)/vmap()/triangular_solve | solution.py:20
  432.8 1.4 convolution_subtract_fusion.3
  438.1 11.7 %custom-call.35 = f32[2,64,64]{2,1,0:T(8,128)S(1)} custom-call(f32[2,64,64]{2,1,0:T(8,128)S(1)} %fusion.26), custom_call_target="Cholesky" | custom-call | tf_op jit(solution)/shard_map/jit(cholesky)/cholesky | solution.py:19
  450.1 10.0 %custom-call.36 = f32[2,1,64,64]{2,3,1,0:T(8,128)S(1)} custom-call(f32[2,1,64,64]{3,2,1,0:T(8,128)S(1)} %select_bitcast_fusion.1), custom_call_target="InvertDiagBlocksLowerTriangular" | custom-call | tf_op jit(solution)/shard_map/jit(_cho_solve)/vmap()/triangular_solve | solution.py:20
  462.9 5.8 %custom-call.37 = f32[1,64,64]{2,1,0:T(8,128)S(1)} custom-call(f32[1,64,64]{2,1,0:T(8,128)S(1)} %fusion.38), custom_call_target="Cholesky" | custom-call | tf_op jit(solution)/shard_map/jit(cholesky)/cholesky | solution.py:19
  470.1 4.9 custom-call.38
  476.6 1.8 convolution_add_fusion.2
  478.4 12.8 %all-gather.11.cloned.1.call-done = f32[64,4096]{1,0:T(8,128)} async-done(((f32[16,4096]{1,0:T(8,128)}), f32[64,4096]{1,0:T(8,128)}) %all-gather.11.cloned.1.call-update) | async-done | bytes 1048592 | tf_op jit(solution)/shard_map/all_gather | solution.py:118
  491.2 1.8 convolution_add_fusion.1
  493.1 57.1 %all-gather.13.cloned.1.call-done = f32[64,4096]{1,0:T(8,128)} async-done(((f32[16,4096]{1,0:T(8,128)}), f32[64,4096]{1,0:T(8,128)}) %all-gather.13.cloned.1.call-update) | async-done | bytes 1048592 | tf_op jit(solution)/shard_map/all_gather | solution.py:119
  550.2 2.5 convolution_add_fusion
  (104 shorter events, 22.8 us)
Async XLA Ops:
  6.5 3.2 copy-start
  6.5 3.1 copy-start.5
  6.5 229.4 %all-gather.15.cloned.1.call-start = ((), (), s32[]{:S(2)}) async-start(), calls=%async_computation.4 | async-start | bytes 12681216 | tf_op jit(solution)/shard_map/all_gather | solution.py:107
  8.6 2.1 copy-start.3
  10.7 1.2 copy-start.4
  13.7 357.0 %all-gather.7.cloned.1.call-start = ((), (), s32[]{:S(2)}) async-start(), calls=%async_computation | async-start | bytes 3932160 | tf_op jit(solution)/shard_map/all_gather | solution.py:110
  243.3 233.3 %all-gather.9.cloned.1.call-start = ((), (), s32[]{:S(2)}) async-start(), calls=%async_computation.1 | async-start | bytes 1310720 | tf_op jit(solution)/shard_map/all_gather | solution.py:117
  244.0 247.2 %all-gather.11.cloned.1.call-start = ((), (), s32[]{:S(2)}) async-start(), calls=%async_computation.2 | async-start | bytes 1310720 | tf_op jit(solution)/shard_map/all_gather | solution.py:118
  244.6 305.6 %all-gather.13.cloned.1.call-start = ((), (), s32[]{:S(2)}) async-start(), calls=%async_computation.3 | async-start | bytes 1310720 | tf_op jit(solution)/shard_map/all_gather | solution.py:119
  379.6 1.2 copy-start.1
  432.8 1.9 copy-start.10
  434.2 1.7 copy-start.6
  434.3 1.7 copy-start.7
  434.3 1.7 copy-start.8
  434.3 1.7 copy-start.9
  460.8 15.8 %copy-start.2 = (f32[16,4096]{1,0:T(8,128)S(1)}, f32[16,4096]{1,0:T(8,128)}, u32[]{:S(2)}) copy-start(f32[16,4096]{1,0:T(8,128)} %param.7) | copy-start | bytes 786436
Sparse Core Ops, SparseCore 0:
  13.8 222.0 all-gather.14
  243.4 127.1 all-gather.6
  372.8 57.1 all-gather.8
  431.9 59.3 all-gather.10
  493.2 56.9 all-gather.12
where the time goes:
time: 560 us; the launch traced here: 559 us
  waiting for transfers between devices  419 us (75%)
  other arithmetic  87.9 us (16%)
  local copies, waits for them, and re-layouts  19.4 us (3%)
  matrix products  18.8 us (3%)
  between operations  13.9 us (2%)
    all_gather x1, waiting for transfers between devices, on_device(): everyone = lax.all_gather(local_terms[None], 'rows', axis=0, tiled=True)  222 us
    all_gather x1, waiting for transfers between devices, on_device(): lax.all_gather(node_terms, 'cols', axis=3, tiled=True)  125 us
    all_gather x1, waiting for transfers between devices, on_device(): lax.all_gather(factor1, 'cols', axis=0, tiled=True)  57.1 us
    another operation x10, other arithmetic, solve_small(): lower_factor = jnp.linalg.cholesky(small_product(turned, matrix))  42.7 us
    another operation x7, other arithmetic, solve_small(): jax.scipy.linalg.cho_solve((lower_factor, True), small_product(turned, ri...  36.1 us
    all_gather x1, waiting for transfers between devices, on_device(): lax.all_gather(factor2, 'cols', axis=0, tiled=True)  12.8 us
  transfers between devices with their start and end apart: 5, of which 4 were waited for; matrix products, arithmetic and copies ran while one was open for 20% of the time, Pallas kernels for 0%

commit v1 on v0

v1 whole, which is shorter than its diff:
```python
import functools

import jax
import jax.numpy as jnp
import numpy as np
from jax import lax
from jax.experimental import pallas as pl
from jax.experimental.pallas import tpu as pltpu
from jax.sharding import Mesh, PartitionSpec as P

RANK = 64
LOCAL = 16
ROWS = 4096
HALF = ROWS // 2
CHUNK = 1024
MESSAGE = 160
LIMIT = 48 * 1024 * 1024

LEAF = ("yl", "x", "core")
SLAB = ("yh", "zl", "zh")
BLOCKS = ("zl", "yh", "yl", "x", "core")
NEAR = [(0, 1), (1, 0), (2, 3), (3, 2)]
FAR = [(0, 3), (3, 0), (1, 2), (2, 1)]

bf16 = jnp.bfloat16
f32 = jnp.float32


def split(values):
    high = values.astype(bf16)
    return high, (values - high.astype(f32)).astype(bf16)


def dot(left, right):
    return jnp.dot(left, right, preferred_element_type=f32)


def exact(left, right):
    return jnp.dot(left, right, precision=lax.Precision.HIGHEST, preferred_element_type=f32)


def products(solves, factor3, factor2, factor1, basis3, basis2, basis1, out, total):
    step = pl.program_id(0)
    dims = (((1,), (1,)), ((), ()))
    stacked = jnp.concatenate([solves[...], factor3[...], factor2[...], factor1[...]], 0)
    high, low = split(stacked)
    both = jnp.concatenate([high, low], 0)

    @pl.when(step == 0)
    def _():
        total[...] = jnp.zeros_like(total)

    for slot, basis in enumerate((basis3, basis2, basis1)):
        top, rest = split(basis[...])
        wide = lax.dot_general(both, top, dims, preferred_element_type=f32)
        thin = lax.dot_general(high, rest, dims, preferred_element_type=f32)
        total[slot] += wide[:RANK] + (wide[RANK:] + thin)

    @pl.when(step == pl.num_programs(0) - 1)
    def _():
        for slot in range(3):
            here = total[slot]
            out[:, 2 * slot, :] = jnp.concatenate([here[0:16], here[32:48]], 1)
            out[:, 2 * slot + 1, :] = jnp.concatenate([here[16:32], here[48:64]], 1)
        out[:, 6, :] = jnp.zeros((16, 128), f32)
        out[:, 7, :] = jnp.zeros((16, 128), f32)


def local_products(*arrays):
    narrow = pl.BlockSpec((LOCAL, CHUNK), lambda i: (0, i))
    wide = pl.BlockSpec((RANK, CHUNK), lambda i: (0, i))
    return pl.pallas_call(
        products,
        grid=(ROWS // CHUNK,),
        in_specs=[narrow] * 4 + [wide] * 3,
        out_specs=pl.BlockSpec((16, 8, 128), lambda i: (0, 0, 0)),
        out_shape=jax.ShapeDtypeStruct((16, 8, 128), f32),
        scratch_shapes=[pltpu.VMEM((3, RANK, RANK), f32)],
        cost_estimate=pl.CostEstimate(
            flops=2 * 3 * 192 * 64 * ROWS, bytes_accessed=ROWS * 256 * 4, transcendentals=0
        ),
    )(*arrays)


def leaf_sum(pieces, out):
    total = pieces[0]
    for index in range(1, 16):
        total = total + pieces[index]
    out[...] = jnp.broadcast_to(total[None], out.shape)


def pack(pieces, out):
    rows = [pieces[:, index, :] for index in range(6)]
    message = jnp.concatenate(
        [
            rows[0],
            rows[1],
            rows[3],
            rows[5],
            rows[2][:16] + rows[2][16:],
            rows[4][:16] + rows[4][16:],
        ],
        0,
    )
    out[...] = jnp.broadcast_to(message[None], out.shape)


def inverses(matrices):
    eye = (
        lax.broadcasted_iota(jnp.int32, (RANK, RANK), 0)
        == lax.broadcasted_iota(jnp.int32, (RANK, RANK), 1)
    ).astype(f32)
    starts = []
    for matrix in matrices:
        size = jnp.abs(matrix)
        by_row = jnp.max(jnp.sum(size, 1, keepdims=True), 0, keepdims=True)
        by_column = jnp.max(jnp.sum(size, 0, keepdims=True), 1, keepdims=True)
        starts.append(matrix.T / by_row / by_column)

    def improve(state):
        count, _, guesses = state
        gaps = [eye - exact(m, g) for m, g in zip(matrices, guesses)]
        worst = gaps[0] * gaps[0]
        for gap in gaps[1:]:
            worst = worst + gap * gap
        better = tuple(g + exact(g, gap) for g, gap in zip(guesses, gaps))
        return count + 1, jnp.sum(worst), better

    def unfinished(state):
        count, error, _ = state
        return (count < 64) & jnp.logical_not(error <= 1e-7)

    state = lax.while_loop(unfinished, improve, (jnp.int32(0), jnp.float32(1.0), tuple(starts)))
    return state[2]


def merge(nodes):
    eye = (
        lax.broadcasted_iota(jnp.int32, (RANK, RANK), 0)
        == lax.broadcasted_iota(jnp.int32, (RANK, RANK), 1)
    ).astype(f32)
    reduced = [eye - exact(kb, ka) for ka, kb, _, _ in nodes]
    sides = [ra - exact(rb, ka) for ka, _, ra, rb in nodes]
    turned = inverses(reduced)
    bottoms = [exact(side, inv) for side, inv in zip(sides, turned)]
    tops = [rb - exact(low, kb) for (_, kb, _, rb), low in zip(nodes, bottoms)]
    return tops, bottoms


def tree(place, sums, near_out, far_out, first, second, third, whole):
    def rows(base, entry):
        return jnp.concatenate(
            [sums[pl.ds(base + entry * 4 + zh, 16, stride=MESSAGE), :] for zh in range(4)], 0
        )

    def left(values):
        return values[:, :RANK]

    def right(values):
        return values[:, RANK:]

    nodes = []
    couple = []
    carry2 = []
    carry1 = []
    for zl in range(4):
        xa, xb = rows(0, zl), rows(0, 4 + zl)
        fa, fb = rows(32, zl), rows(32, 4 + zl)
        nodes.append(
            (
                left(fa),
                left(fb),
                jnp.concatenate([left(xa), right(xa), right(fa)], 0),
                jnp.concatenate([left(xb), right(xb), right(fb)], 0),
            )
        )
        ga, gb = rows(64, zl), rows(64, 4 + zl)
        ha, hb = rows(96, zl), rows(96, 4 + zl)
        x2, x1 = rows(128, zl), rows(144, zl)
        couple.append(
            (
                jnp.concatenate([left(ga), left(ha)], 1),
                jnp.concatenate([left(gb), left(hb)], 1),
            )
        )
        carry2.append(jnp.concatenate([left(x2), right(x2), right(ga) + right(gb)], 0))
        carry1.append(jnp.concatenate([left(x1), right(x1), right(ha) + right(hb)], 0))
    tops, bottoms = merge(nodes)
    two = []
    one = []
    for zl in range(4):
        third[2 * zl] = tops[zl]
        third[2 * zl + 1] = bottoms[zl]
        update = exact(tops[zl], couple[zl][0]) + exact(bottoms[zl], couple[zl][1])
        two.append(carry2[zl] - left(update))
        one.append(carry1[zl] - right(update))

    def keep(values):
        return jnp.concatenate([values[:RANK], values[2 * RANK :]], 0)

    nodes = [
        (
            two[2 * m][RANK : 2 * RANK],
            two[2 * m + 1][RANK : 2 * RANK],
            keep(two[2 * m]),
            keep(two[2 * m + 1]),
        )
        for m in range(2)
    ]
    tops, bottoms = merge(nodes)
    last = []
    for m in range(2):
        second[2 * m] = tops[m]
        second[2 * m + 1] = bottoms[m]
        last.append(
            keep(one[2 * m])
            + keep(one[2 * m + 1])
            - exact(tops[m], one[2 * m][RANK : 2 * RANK])
            - exact(bottoms[m], one[2 * m + 1][RANK : 2 * RANK])
        )
    tops, bottoms = merge([(last[0][RANK:], last[1][RANK:], last[0][:RANK], last[1][:RANK])])
    first[0] = tops[0]
    first[1] = bottoms[0]

    zl, yh, zh = place[0], place[1], place[2]
    near = place[3]
    far = place[4]
    c3 = third[2 * zl + yh]
    c2 = second[zl]
    d1 = first[zl // 2]
    d2 = c2[:RANK] - exact(d1, c2[RANK:])
    d3 = c3[:RANK] - exact(d2, c3[RANK : 2 * RANK]) - exact(d1, c3[2 * RANK :])
    whole[...] = jnp.concatenate([d3, d2, d1], 1)

    def chosen(partner, target):
        picked = jnp.concatenate(
            [whole[pl.ds(zh * 16, 16), :], whole[pl.ds(target * 16, 16), :]], 0
        )
        source = lax.broadcasted_iota(jnp.int32, (192, 96), 0)
        column = lax.broadcasted_iota(jnp.int32, (192, 96), 1)
        owner = jnp.where(column < 48, zh, partner)
        inner = jnp.where(column < 48, column, column - 48)
        wanted = (inner // 16) * RANK + owner * 16 + inner % 16
        return -exact(picked, (source == wanted).astype(f32))

    near_out[...] = chosen(near, far)
    far_out[...] = chosen(far, near)


def apply_rows(coefficient, own, other):
    high, low = split(coefficient)
    both = jnp.concatenate([high, low], 0)
    factor = jnp.concatenate([own, other], 0)
    top, rest = split(factor)
    wide = dot(both, top)
    return wide[:16] + (wide[16:] + dot(high, rest))


def outgoing(near_c, far_c, own_a, own_b, got_a, got_b, out_a, out_b):
    out_a[...] = apply_rows(near_c[16:], own_a[...], got_a[...])
    out_b[...] = apply_rows(far_c[16:], own_b[...], got_b[...])


def staying(near_c, far_c, own_a, own_b, got_a, got_b, solves, out):
    out[:, :HALF] = solves[:, :HALF] + apply_rows(near_c[:16], own_a[...], got_a[...])
    out[:, HALF:] = solves[:, HALF:] + apply_rows(far_c[:16], own_b[...], got_b[...])


def call(kernel, shapes, *arrays, scratch=(), **kwargs):
    return pl.pallas_call(
        kernel,
        out_shape=shapes,
        scratch_shapes=list(scratch),
        compiler_params=pltpu.CompilerParams(vmem_limit_bytes=LIMIT),
        **kwargs,
    )(*arrays)


def shape(*dims):
    return jax.ShapeDtypeStruct(dims, f32)


def on_device(solves, factor3, factor2, factor1, basis3, basis2, basis1):
    zh = lax.axis_index("zh")
    own_a = jnp.concatenate([factor3[:, :HALF], factor2[:, :HALF], factor1[:, :HALF]], 0)
    own_b = jnp.concatenate([factor3[:, HALF:], factor2[:, HALF:], factor1[:, HALF:]], 0)
    got_a = lax.ppermute(own_a, "zh", NEAR)
    got_b = lax.ppermute(own_b, "zh", FAR)
    slots = local_products(solves, factor3, factor2, factor1, basis3, basis2, basis1)
    pieces = lax.all_to_all(slots, LEAF, 0, 0, tiled=True)
    copies = call(leaf_sum, shape(32, 8, 128), pieces)
    slabs = lax.all_to_all(copies, SLAB, 0, 0, tiled=True)
    message = call(pack, shape(16, MESSAGE, 128), slabs)
    sums = lax.all_to_all(message, LEAF, 0, 0, tiled=True).reshape(16 * MESSAGE, 128)
    place = jnp.stack(
        [lax.axis_index("zl"), lax.axis_index("yh"), zh, zh ^ 1, 3 - zh]
    ).astype(jnp.int32)
    vmem = pl.BlockSpec(memory_space=pltpu.VMEM)
    near_c, far_c = call(
        tree,
        (shape(32, 96), shape(32, 96)),
        place,
        sums,
        in_specs=[pl.BlockSpec(memory_space=pltpu.SMEM), vmem],
        out_specs=(vmem, vmem),
        scratch=[
            pltpu.VMEM((2, 64, 64), f32),
            pltpu.VMEM((4, 128, 64), f32),
            pltpu.VMEM((8, 192, 64), f32),
            pltpu.VMEM((64, 192), f32),
        ],
    )
    blocks = (near_c, far_c, own_a, own_b, got_a, got_b)
    cost = pl.CostEstimate(flops=2 * 3 * 96 * 16 * ROWS, bytes_accessed=96 * ROWS * 4, transcendentals=0)
    send_a, send_b = call(outgoing, (shape(16, HALF), shape(16, HALF)), *blocks, cost_estimate=cost)
    came_a = lax.ppermute(send_a, "zh", FAR)
    came_b = lax.ppermute(send_b, "zh", NEAR)
    kept = call(staying, shape(16, ROWS), *blocks, solves, cost_estimate=cost)
    return kept + jnp.concatenate([came_a, came_b], 1)


def solution(mesh):
    fine = Mesh(
        mesh.devices.reshape(4, 2, 2, 4, 2, 4), ("zl", "yh", "yl", "x", "core", "zh")
    )
    split_both = P("zh", BLOCKS)
    split_rows = P(None, BLOCKS)
    return jax.shard_map(
        on_device,
        mesh=fine,
        in_specs=(split_both,) * 4 + (split_rows,) * 3,
        out_specs=split_both,
        check_vma=False,
    )
```

time: 560 us -> 125 us (0.22)
  the two profiles are of different devices: /device:TPU:1 before, /device:TPU:2 now
where the time goes in v1:
time: 125 us; the launch traced here: 124 us
  waiting for transfers between devices  48.4 us (39%)
  starting transfers between devices  39.5 us (32%)
  Pallas kernels  21.2 us (17%)
  blocking collectives  14 us (11%)
    pallas_call x5, Pallas kernels, call(): pl.pallas_call(kernel, out_shape=shapes, scratch_shapes=list(scratch), co...  16.3 us
    all_to_all x1, waiting for transfers between devices, on_device(): slabs = lax.all_to_all(copies, SLAB, 0, 0, tiled=True)  15.5 us
    all_to_all x1, starting transfers between devices, on_device(): slabs = lax.all_to_all(copies, SLAB, 0, 0, tiled=True)  14.4 us
    all_to_all x1, blocking collectives, on_device(): pieces = lax.all_to_all(slots, LEAF, 0, 0, tiled=True)  14 us
    ppermute x1, waiting for transfers between devices, on_device(): got_b = lax.ppermute(own_b, 'zh', FAR)  12.2 us
    ppermute x1, waiting for transfers between devices, on_device(): came_b = lax.ppermute(send_b, 'zh', NEAR)  12.1 us
    all_to_all x1, waiting for transfers between devices, on_device(): lax.all_to_all(message, LEAF, 0, 0, tiled=True).reshape(16 * MESSAGE, 128)  8.49 us
    ppermute x1, starting transfers between devices, on_device(): came_a = lax.ppermute(send_a, 'zh', FAR)  8.29 us
  transfers between devices with their start and end apart: 6, of which 4 were waited for; matrix products, arithmetic and copies ran while one was open for 0% of the time, Pallas kernels for 11%

profile of v1, /device:TPU:2, one launch (start us, length us, event | category | flops | bytes accessed | tf_op | source)
XLA Modules:
  0.0 124.2 jit_solution(16538314583421021049)
XLA Ops:
  0.0 4.9 %shard_map.73 = f32[16,8,128]{2,1,0:T(8,128)} custom-call(f32[16,4096]{1,0:T(8,128)} %solves.3, f32[16,4096]{1,0:T(8,128)} %factor3.1, f32[16,4096]{1,0:T(8,128)} %factor2.1, f32[16,4096]{1,0:T(8,128)} %factor1.1, f32[64,4096]{1,0:T(8,128)} %basis3.1, f32[64,4096]{1,0:T(8,128)} %basis2.1, f32[64,4096]{1,0:T(8,128)} %basis1.1), custom_call_target="tpu_custom_call" | custom-call | flops 301989888 | bytes 4194304 | tf_op jit(solution)/shard_map/pallas_call | solution.py:72
  4.9 14.0 %all_to_all.15.pieces = f32[16,8,128]{2,1,0:T(8,128)S(1)} all-to-all(f32[16,8,128]{2,1,0:T(8,128)} %shard_map.73), channel_id=1, replica_groups=mesh['zl'=4,'yh'=2,'yl'=2,'x'=4,'core'=2,'zh'=4] {'yl','x','core'}, dimensions={0} | all-to-all | bytes 131072 | tf_op jit(solution)/shard_map/all_to_all | solution.py:290
  18.9 0.7 shard_map.74
  19.6 14.4 %all-to-all-start.1 = ((f32[32,8,128]{2,1,0:T(8,128)}), f32[32,8,128]{2,1,0:T(8,128)S(1)}, u32[]{:S(2)}, u32[]{:S(2)}) async-start(f32[32,8,128]{2,1,0:T(8,128)} %shard_map.74), calls=%async_computation.1 | async-start | bytes 262144 | tf_op jit(solution)/shard_map/all_to_all | solution.py:292
  34.0 0.0 copy-done.2
  34.0 0.0 copy-done.3
  34.1 15.5 %all-to-all-done.1.pieces = f32[32,8,128]{2,1,0:T(8,128)S(1)} async-done(((f32[32,8,128]{2,1,0:T(8,128)}), f32[32,8,128]{2,1,0:T(8,128)S(1)}, u32[]{:S(2)}, u32[]{:S(2)}) %all-to-all-start.1) | async-done | bytes 131104 | tf_op jit(solution)/shard_map/all_to_all | solution.py:292
  49.6 1.2 shard_map.75
  50.8 5.1 %all-to-all-start.2 = ((f32[16,160,128]{2,1,0:T(8,128)}), f32[16,160,128]{2,1,0:T(8,128)S(1)}, u32[]{:S(2)}, u32[]{:S(2)}) async-start(f32[16,160,128]{2,1,0:T(8,128)} %shard_map.75), calls=%async_computation.2 | async-start | bytes 2621440 | tf_op jit(solution)/shard_map/all_to_all | solution.py:294
  55.9 0.0 copy-done.1
  56.0 6.0 %collective-permute-start = (f32[48,2048]{1,0:T(8,128)S(1)}, f32[48,2048]{1,0:T(8,128)S(1)}, u32[]{:S(2)}, u32[]{:S(2)}) collective-permute-start(f32[48,2048]{1,0:T(8,128)S(1)} %pad_maximum_fusion.own_a), channel_id=1, source_target_pairs={{0,1},{1,0},{2,3},{3,2},{4,5},{5,4},{6,7},{7,6},{8,9},{9,8},{10,11... | collective-permute-start | bytes 1179656 | tf_op jit(solution)/shard_map/ppermute | solution.py:287
  62.0 2.2 %collective-permute-start.1 = (f32[48,2048]{1,0:T(8,128)S(1)}, f32[48,2048]{1,0:T(8,128)S(1)}, u32[]{:S(2)}, u32[]{:S(2)}) collective-permute-start(f32[48,2048]{1,0:T(8,128)S(1)} %pad_maximum_fusion.1.own_b), channel_id=1, source_target_pairs={{0,3},{3,0},{1,2},{2,1},{4,7},{7,4},{5,6},{6,5},{8,11},{11,8},{9,1... | collective-permute-start | bytes 1179656 | tf_op jit(solution)/shard_map/ppermute | solution.py:288
  64.2 0.1 stack.23.place
  64.3 8.5 %all-to-all-done.2 = f32[16,160,128]{2,1,0:T(8,128)S(1)} async-done(((f32[16,160,128]{2,1,0:T(8,128)}), f32[16,160,128]{2,1,0:T(8,128)S(1)}, u32[]{:S(2)}, u32[]{:S(2)}) %all-to-all-start.2) | async-done | bytes 1310752 | tf_op jit(solution)/shard_map/all_to_all | solution.py:294
  72.8 13.6 %shard_map.76 = (f32[32,96]{1,0:T(8,128)S(1)}, f32[32,96]{1,0:T(8,128)S(1)}) custom-call(s32[5]{0:T(128)S(1)} %stack.23.place, f32[2560,128]{1,0:T(8,128)S(1)} %bitcast.6), custom_call_target="tpu_custom_call" | custom-call | tf_op jit(solution)/shard_map/pallas_call | solution.py:270
  86.5 0.0 collective-permute-done.got_a
  86.5 12.2 %collective-permute-done.1.got_b = f32[48,2048]{1,0:T(8,128)S(1)} collective-permute-done((f32[48,2048]{1,0:T(8,128)S(1)}, f32[48,2048]{1,0:T(8,128)S(1)}, u32[]{:S(2)}, u32[]{:S(2)}) %collective-permute-start.1) | collective-permute-done | bytes 393248 | tf_op jit(solution)/shard_map/ppermute | solution.py:288
  98.7 0.4 shard_map.78
  99.1 8.3 %collective-permute-start.2 = (f32[16,2048]{1,0:T(8,128)S(1)}, f32[16,2048]{1,0:T(8,128)S(1)}, u32[]{:S(2)}, u32[]{:S(2)}) collective-permute-start(f32[16,2048]{1,0:T(8,128)S(1)} %get-tuple-element.11), channel_id=1, source_target_pairs={{0,3},{3,0},{1,2},{2,1},{4,7},{7,4},{5,6},{6,5},{8,11},{11,8},{9,1... | collective-permute-start | bytes 393224 | tf_op jit(solution)/shard_map/ppermute | solution.py:316
  107.4 3.6 %collective-permute-start.3 = (f32[16,2048]{1,0:T(8,128)S(1)}, f32[16,2048]{1,0:T(8,128)S(1)}, u32[]{:S(2)}, u32[]{:S(2)}) collective-permute-start(f32[16,2048]{1,0:T(8,128)S(1)} %get-tuple-element.12), channel_id=1, source_target_pairs={{0,1},{1,0},{2,3},{3,2},{4,5},{5,4},{6,7},{7,6},{8,9},{9,8},{10,11... | collective-permute-start | bytes 393224 | tf_op jit(solution)/shard_map/ppermute | solution.py:317
  111.0 0.4 shard_map.77
  111.4 0.0 collective-permute-done.2
  111.4 12.1 %collective-permute-done.3 = f32[16,2048]{1,0:T(8,128)S(1)} collective-permute-done((f32[16,2048]{1,0:T(8,128)S(1)}, f32[16,2048]{1,0:T(8,128)S(1)}, u32[]{:S(2)}, u32[]{:S(2)}) %collective-permute-start.3) | collective-permute-done | bytes 131104 | tf_op jit(solution)/shard_map/ppermute | solution.py:317
  123.5 0.7 maximum_add_fusion
  (9 shorter events, 0.1 us)
Async XLA Ops:
  0.0 34.0 %copy-start.2 = (f32[16,4096]{1,0:T(8,128)S(1)}, f32[16,4096]{1,0:T(8,128)}, u32[]{:S(2)}) copy-start(f32[16,4096]{1,0:T(8,128)} %factor3.1) | copy-start | bytes 786436
  0.0 34.0 %copy-start.3 = (f32[16,4096]{1,0:T(8,128)S(1)}, f32[16,4096]{1,0:T(8,128)}, u32[]{:S(2)}) copy-start(f32[16,4096]{1,0:T(8,128)} %factor2.1) | copy-start | bytes 786436
  19.6 30.0 %all-to-all-start.1 = ((f32[32,8,128]{2,1,0:T(8,128)}), f32[32,8,128]{2,1,0:T(8,128)S(1)}, u32[]{:S(2)}, u32[]{:S(2)}) async-start(f32[32,8,128]{2,1,0:T(8,128)} %shard_map.74), calls=%async_computation.1 | async-start | bytes 262144 | tf_op jit(solution)/shard_map/all_to_all | solution.py:292
  50.8 5.1 %copy-start.1 = (f32[16,4096]{1,0:T(8,128)S(1)}, f32[16,4096]{1,0:T(8,128)}, u32[]{:S(2)}) copy-start(f32[16,4096]{1,0:T(8,128)} %factor1.1) | copy-start | bytes 786436
  50.8 22.0 %all-to-all-start.2 = ((f32[16,160,128]{2,1,0:T(8,128)}), f32[16,160,128]{2,1,0:T(8,128)S(1)}, u32[]{:S(2)}, u32[]{:S(2)}) async-start(f32[16,160,128]{2,1,0:T(8,128)} %shard_map.75), calls=%async_computation.2 | async-start | bytes 2621440 | tf_op jit(solution)/shard_map/all_to_all | solution.py:294
  56.0 30.5 %collective-permute-start = (f32[48,2048]{1,0:T(8,128)S(1)}, f32[48,2048]{1,0:T(8,128)S(1)}, u32[]{:S(2)}, u32[]{:S(2)}) collective-permute-start(f32[48,2048]{1,0:T(8,128)S(1)} %pad_maximum_fusion.own_a), channel_id=1, source_target_pairs={{0,1},{1,0},{2,3},{3,2},{4,5},{5,4},{6,7},{7,6},{8,9},{9,8},{10,11... | collective-permute-start | bytes 1179656 | tf_op jit(solution)/shard_map/ppermute | solution.py:287
  62.0 36.7 %collective-permute-start.1 = (f32[48,2048]{1,0:T(8,128)S(1)}, f32[48,2048]{1,0:T(8,128)S(1)}, u32[]{:S(2)}, u32[]{:S(2)}) collective-permute-start(f32[48,2048]{1,0:T(8,128)S(1)} %pad_maximum_fusion.1.own_b), channel_id=1, source_target_pairs={{0,3},{3,0},{1,2},{2,1},{4,7},{7,4},{5,6},{6,5},{8,11},{11,8},{9,1... | collective-permute-start | bytes 1179656 | tf_op jit(solution)/shard_map/ppermute | solution.py:288
  72.8 38.1 %copy-start = (f32[16,4096]{1,0:T(8,128)S(1)}, f32[16,4096]{1,0:T(8,128)}, u32[]{:S(2)}) copy-start(f32[16,4096]{1,0:T(8,128)} %solves.3) | copy-start | bytes 786436
  99.1 12.3 %collective-permute-start.2 = (f32[16,2048]{1,0:T(8,128)S(1)}, f32[16,2048]{1,0:T(8,128)S(1)}, u32[]{:S(2)}, u32[]{:S(2)}) collective-permute-start(f32[16,2048]{1,0:T(8,128)S(1)} %get-tuple-element.11), channel_id=1, source_target_pairs={{0,3},{3,0},{1,2},{2,1},{4,7},{7,4},{5,6},{6,5},{8,11},{11,8},{9,1... | collective-permute-start | bytes 393224 | tf_op jit(solution)/shard_map/ppermute | solution.py:316
  107.4 16.1 %collective-permute-start.3 = (f32[16,2048]{1,0:T(8,128)S(1)}, f32[16,2048]{1,0:T(8,128)S(1)}, u32[]{:S(2)}, u32[]{:S(2)}) collective-permute-start(f32[16,2048]{1,0:T(8,128)S(1)} %get-tuple-element.12), channel_id=1, source_target_pairs={{0,1},{1,0},{2,3},{3,2},{4,5},{5,4},{6,7},{7,6},{8,9},{9,8},{10,11... | collective-permute-start | bytes 393224 | tf_op jit(solution)/shard_map/ppermute | solution.py:317

commit v2 on v1

v2 whole, which is shorter than its diff:
```python
import functools

import jax
import jax.numpy as jnp
import numpy as np
from jax import lax
from jax.experimental import pallas as pl
from jax.experimental.pallas import tpu as pltpu
from jax.sharding import Mesh, PartitionSpec as P

RANK = 64
LOCAL = 16
ROWS = 4096
CHUNK = 1024
MESSAGE = 144
LIMIT = 48 * 1024 * 1024

LEAF = ("yl", "x", "core")
SLAB = ("yh", "zl", "zh")
BLOCKS = ("zl", "yh", "yl", "x", "core")
PAIRS = ("core", "zh")
SWAP = [(0, 1), (1, 0), (2, 3), (3, 2), (4, 7), (7, 4), (5, 6), (6, 5)]
RETURN = [(0, 3), (3, 0), (1, 2), (2, 1), (4, 5), (5, 4), (6, 7), (7, 6)]

bf16 = jnp.bfloat16
f32 = jnp.float32


def split(values):
    high = values.astype(bf16)
    return high, (values - high.astype(f32)).astype(bf16)


def dot(left, right):
    return jnp.dot(left, right, preferred_element_type=f32)


def exact(left, right):
    return full(left, right)


FREE = pl.CostEstimate(flops=0, bytes_accessed=0, transcendentals=0)


def full(left, right):
    count = left.shape[0]
    top, middle = split(left)
    low = (left - top.astype(f32) - middle.astype(f32)).astype(bf16)
    right_top, right_middle = split(right)
    right_low = (right - right_top.astype(f32) - right_middle.astype(f32)).astype(bf16)
    first = dot(jnp.concatenate([top, middle, low], 0), right_top)
    second = dot(jnp.concatenate([top, middle], 0), right_middle)
    third = dot(top, right_low)
    small = first[2 * count :] + second[count:] + third
    return first[:count] + (first[count : 2 * count] + second[:count] + small)


def products(
    solves, factor3, factor2, factor1, basis3, basis2, basis1, out, own, total3, total21
):
    step = pl.program_id(0)
    dims = (((1,), (1,)), ((), ()))
    factors = jnp.concatenate([factor2[...], factor1[...]], 0)
    own[...] = factors
    high, low = split(jnp.concatenate([solves[...], factor3[...], factors], 0))
    both = jnp.concatenate([high, low], 0)

    @pl.when(step == 0)
    def _():
        total3[...] = jnp.zeros_like(total3)
        total21[...] = jnp.zeros_like(total21)

    for total, basis in (
        (total3, basis3[...]),
        (total21, jnp.concatenate([basis2[...], basis1[...]], 0)),
    ):
        top, rest = split(basis)
        wide = lax.dot_general(both, top, dims, preferred_element_type=f32)
        thin = lax.dot_general(high, rest, dims, preferred_element_type=f32)
        total[...] += wide[:RANK] + (wide[RANK:] + thin)

    @pl.when(step == pl.num_programs(0) - 1)
    def _():
        deep = total3[...]
        out[:, 0, :] = jnp.concatenate([deep[0:16], deep[32:48]], 1)
        out[:, 1, :] = jnp.concatenate([deep[16:32], deep[48:64]], 1)
        out[:, 2, :] = total21[16:32, :]
        out[:, 3, :] = total21[0:16, :]
        out[:, 4, :] = total21[32:48, :]
        out[:, 5, :] = total21[48:64, :]
        out[:, 6, :] = jnp.zeros((16, 128), f32)
        out[:, 7, :] = jnp.zeros((16, 128), f32)


def local_products(*arrays):
    narrow = pl.BlockSpec((LOCAL, CHUNK), lambda i: (0, i))
    wide = pl.BlockSpec((RANK, CHUNK), lambda i: (0, i))
    return pl.pallas_call(
        products,
        grid=(ROWS // CHUNK,),
        in_specs=[narrow] * 4 + [wide] * 3,
        out_specs=(
            pl.BlockSpec((16, 8, 128), lambda i: (0, 0, 0)),
            pl.BlockSpec((2 * LOCAL, CHUNK), lambda i: (0, i)),
        ),
        out_shape=(shape(16, 8, 128), shape(2 * LOCAL, ROWS)),
        scratch_shapes=[pltpu.VMEM((RANK, RANK), f32), pltpu.VMEM((RANK, 2 * RANK), f32)],
        cost_estimate=FREE,
    )(*arrays)


def leaf_sum(pieces, out):
    total = pieces[0]
    for index in range(1, 16):
        total = total + pieces[index]
    out[...] = jnp.broadcast_to(total[None], out.shape)


def pack(pieces, out):
    rows = [pieces[:, index, :] for index in range(6)]
    paired = [rows[index][:16] + rows[index][16:] for index in (3, 4, 5)]
    message = jnp.concatenate(rows[:3] + paired, 0)
    out[...] = jnp.broadcast_to(message[None], out.shape)


def identity():
    return (
        lax.broadcasted_iota(jnp.int32, (RANK, RANK), 0)
        == lax.broadcasted_iota(jnp.int32, (RANK, RANK), 1)
    ).astype(f32)


def squares(matrices):
    total = matrices[0] * matrices[0]
    for matrix in matrices[1:]:
        total = total + matrix * matrix
    return jnp.sum(total)


def inverses(crossed, scratch):
    eye = identity()
    size = squares(crossed)
    close = size < 0.8

    @pl.when(close)
    def _():
        def improve(state):
            powers, guesses, _ = state
            both = [full(jnp.concatenate([e, g], 0), e) for g, e in zip(guesses, powers)]
            better = tuple(g + b[RANK:] for g, b in zip(guesses, both))
            return tuple(b[:RANK] for b in both), better, squares(powers)

        def unfinished(state):
            return state[2] > 1e-8

        first = tuple(full(e, e) for e in crossed)
        state = lax.while_loop(
            unfinished, improve, (first, tuple(eye + e for e in crossed), size)
        )
        for index, guess in enumerate(state[1]):
            scratch[index] = guess

    @pl.when(jnp.logical_not(close))
    def _():
        matrices = [eye - e for e in crossed]
        starts = []
        for matrix in matrices:
            level = jnp.abs(matrix)
            by_row = jnp.max(jnp.sum(level, 1, keepdims=True), 0, keepdims=True)
            by_column = jnp.max(jnp.sum(level, 0, keepdims=True), 1, keepdims=True)
            starts.append(matrix.T / by_row / by_column)

        def improve(state):
            count, _, guesses = state
            gaps = [eye - exact(m, g) for m, g in zip(matrices, guesses)]
            better = tuple(g + exact(g, gap) for g, gap in zip(guesses, gaps))
            return count + 1, squares(gaps), better

        def unfinished(state):
            count, error, _ = state
            return (count < 64) & jnp.logical_not(error <= 1e-7)

        state = lax.while_loop(
            unfinished, improve, (jnp.int32(0), jnp.float32(1.0), tuple(starts))
        )
        for index, guess in enumerate(state[2]):
            scratch[index] = guess


def merge(nodes, scratch):
    crossed = [exact(kb, ka) for ka, kb, _, _ in nodes]
    sides = [ra - exact(rb, ka) for ka, _, ra, rb in nodes]
    inverses(crossed, scratch)
    bottoms = [exact(side, scratch[index]) for index, side in enumerate(sides)]
    tops = [rb - exact(low, kb) for (_, kb, _, rb), low in zip(nodes, bottoms)]
    return tops, bottoms


def tree(place, sums, out, first, second, third, whole, solved):
    def rows(base, entry):
        return jnp.concatenate(
            [sums[pl.ds(base + entry * 4 + zh, 16, stride=MESSAGE), :] for zh in range(4)], 0
        )

    def left(values):
        return values[:, :RANK]

    def right(values):
        return values[:, RANK:]

    nodes = []
    couple = []
    carry = []
    for zl in range(4):
        xa, xb = rows(0, zl), rows(0, 4 + zl)
        fa, fb = rows(32, zl), rows(32, 4 + zl)
        nodes.append(
            (
                left(fa),
                left(fb),
                jnp.concatenate([left(xa), right(xa), right(fa)], 0),
                jnp.concatenate([left(xb), right(xb), right(fb)], 0),
            )
        )
        couple.append((rows(64, zl), rows(64, 4 + zl)))
        carry.append(jnp.concatenate([rows(96, zl), rows(112, zl), rows(128, zl)], 0))
    tops, bottoms = merge(nodes, solved)
    two = []
    one = []
    for zl in range(4):
        third[2 * zl] = tops[zl]
        third[2 * zl + 1] = bottoms[zl]
        update = exact(tops[zl], couple[zl][0]) + exact(bottoms[zl], couple[zl][1])
        carried = carry[zl] - update
        two.append(left(carried))
        one.append(right(carried))

    def keep(values):
        return jnp.concatenate([values[:RANK], values[2 * RANK :]], 0)

    nodes = [
        (
            two[2 * m][RANK : 2 * RANK],
            two[2 * m + 1][RANK : 2 * RANK],
            keep(two[2 * m]),
            keep(two[2 * m + 1]),
        )
        for m in range(2)
    ]
    tops, bottoms = merge(nodes, solved)
    last = []
    for m in range(2):
        second[2 * m] = tops[m]
        second[2 * m + 1] = bottoms[m]
        last.append(
            keep(one[2 * m])
            + keep(one[2 * m + 1])
            - exact(tops[m], one[2 * m][RANK : 2 * RANK])
            - exact(bottoms[m], one[2 * m + 1][RANK : 2 * RANK])
        )
    tops, bottoms = merge([(last[0][RANK:], last[1][RANK:], last[0][:RANK], last[1][:RANK])], solved)
    first[0] = tops[0]
    first[1] = bottoms[0]

    zl, yh, zh = place[0], place[1], place[2]
    partner = place[3]
    target = place[4]
    c3 = third[2 * zl + yh]
    c2 = second[zl]
    d1 = first[zl // 2]
    d2 = c2[:RANK] - exact(d1, c2[RANK:])
    d3 = c3[:RANK] - exact(d2, c3[RANK : 2 * RANK]) - exact(d1, c3[2 * RANK :])
    whole[...] = jnp.concatenate([d3, d2, d1], 1)

    picked = jnp.concatenate(
        [whole[pl.ds(zh * 16, 16), :], whole[pl.ds(target * 16, 16), :]], 0
    )
    source = lax.broadcasted_iota(jnp.int32, (192, 128), 0)
    column = lax.broadcasted_iota(jnp.int32, (192, 128), 1)
    owner = jnp.where(column < 48, zh, partner)
    inner = jnp.where(column < 48, column, column - 48)
    wanted = (inner // 16) * RANK + owner * 16 + inner % 16
    out[...] = -exact(picked, ((source == wanted) & (column < 96)).astype(f32))


def apply_rows(coefficient, *factors):
    high, low = split(coefficient)
    both = jnp.concatenate([high, low], 0)
    top, rest = split(jnp.concatenate([factor[...] for factor in factors], 0))
    wide = dot(both, top)
    return wide[:16] + (wide[16:] + dot(high, rest))


def outgoing(weights, own3, own, got3, got, out):
    out[...] = apply_rows(weights[16:32, :96], own3, own, got3, got)


def staying(weights, own3, own, got3, got, solves, out):
    out[...] = solves[...] + apply_rows(weights[0:16, :96], own3, own, got3, got)


def call(kernel, shapes, *arrays, scratch=(), **kwargs):
    return pl.pallas_call(
        kernel,
        out_shape=shapes,
        scratch_shapes=list(scratch),
        compiler_params=pltpu.CompilerParams(vmem_limit_bytes=LIMIT),
        cost_estimate=FREE,
        **kwargs,
    )(*arrays)


def shape(*dims):
    return jax.ShapeDtypeStruct(dims, f32)


def on_device(solves, factor3, factor2, factor1, basis3, basis2, basis1):
    zh = lax.axis_index("zh")
    core = lax.axis_index("core")
    near, far = zh ^ 1, 3 - zh
    place = jnp.stack(
        [
            lax.axis_index("zl"),
            lax.axis_index("yh"),
            zh,
            jnp.where(core == 0, near, far),
            jnp.where(core == 0, far, near),
        ]
    ).astype(jnp.int32)
    got3 = lax.ppermute(factor3, PAIRS, SWAP)
    slots, own = local_products(solves, factor3, factor2, factor1, basis3, basis2, basis1)
    slots, place = lax.optimization_barrier((slots, place))
    got = lax.ppermute(own, PAIRS, SWAP)
    pieces = lax.all_to_all(slots, LEAF, 0, 0, tiled=True)
    vmem = pl.BlockSpec(memory_space=pltpu.VMEM)

    copies = call(leaf_sum, shape(32, 8, 128), pieces)
    copies, got3 = lax.optimization_barrier((copies, got3))
    slabs = lax.all_to_all(copies, SLAB, 0, 0, tiled=True)
    message = call(pack, shape(16, MESSAGE, 128), slabs)
    sums = lax.all_to_all(message, LEAF, 0, 0, tiled=True).reshape(16 * MESSAGE, 128)
    coefficients = call(
        tree,
        shape(32, 128),
        place,
        sums,
        in_specs=[pl.BlockSpec(memory_space=pltpu.SMEM), vmem],
        out_specs=vmem,
        scratch=[
            pltpu.VMEM((2, 64, 64), f32),
            pltpu.VMEM((4, 128, 64), f32),
            pltpu.VMEM((8, 192, 64), f32),
            pltpu.VMEM((64, 192), f32),
            pltpu.VMEM((4, 64, 64), f32),
        ],
    )
    sent = call(outgoing, shape(16, ROWS), coefficients, factor3, own, got3, got)
    came = lax.ppermute(sent, PAIRS, RETURN)
    return call(staying, shape(16, ROWS), coefficients, factor3, own, got3, got, solves) + came


def solution(mesh):
    fine = Mesh(
        mesh.devices.reshape(4, 2, 2, 4, 2, 4), ("zl", "yh", "yl", "x", "core", "zh")
    )
    split_both = P("zh", BLOCKS)
    split_rows = P(None, BLOCKS)
    return jax.shard_map(
        on_device,
        mesh=fine,
        in_specs=(split_both,) * 4 + (split_rows,) * 3,
        out_specs=split_both,
        check_vma=False,
    )
```

time: 125 us -> 112 us (0.90)
  the two profiles are of different devices: /device:TPU:2 before, /device:TPU:1 now
where the time goes in v2:
time: 112 us; the launch traced here: 111 us
  blocking collectives  34.8 us (31%)
  starting transfers between devices  29.8 us (27%)
  waiting for transfers between devices  27 us (24%)
  Pallas kernels  18.9 us (17%)
    all_to_all x1, blocking collectives, on_device(): slabs = lax.all_to_all(copies, SLAB, 0, 0, tiled=True)  23.5 us
    ppermute x1, waiting for transfers between devices, on_device(): came = lax.ppermute(sent, PAIRS, RETURN)  14.1 us
    pallas_call x5, Pallas kernels, call(): pl.pallas_call(kernel, out_shape=shapes, scratch_shapes=list(scratch), co...  14 us
    ppermute x1, starting transfers between devices, on_device(): got3 = lax.ppermute(factor3, PAIRS, SWAP)  13.3 us
    all_to_all x1, waiting for transfers between devices, on_device(): lax.all_to_all(message, LEAF, 0, 0, tiled=True).reshape(16 * MESSAGE, 128)  12.8 us
    all_to_all x1, blocking collectives, on_device(): pieces = lax.all_to_all(slots, LEAF, 0, 0, tiled=True)  11.3 us
    all_to_all x1, starting transfers between devices, on_device(): lax.all_to_all(message, LEAF, 0, 0, tiled=True).reshape(16 * MESSAGE, 128)  7.32 us
    pallas_call x1, Pallas kernels, local_products(): pl.pallas_call(products, grid=(ROWS // CHUNK,), in_specs=[narrow] * 4 + [...  4.88 us
  transfers between devices with their start and end apart: 4, of which 2 were waited for; matrix products, arithmetic and copies ran while one was open for 0% of the time, Pallas kernels for 16%

profile of v2, /device:TPU:1, one launch (start us, length us, event | category | flops | bytes accessed | tf_op | source)
XLA Modules:
  0.0 111.3 jit_solution(11286681046830045569)
XLA Ops:
  0.0 13.3 %collective-permute-start = (f32[16,4096]{1,0:T(8,128)}, f32[16,4096]{1,0:T(8,128)S(1)}, u32[]{:S(2)}, u32[]{:S(2)}) collective-permute-start(f32[16,4096]{1,0:T(8,128)} %own3.3), channel_id=1, source_target_pairs={{0,1},{1,0},{2,3},{3,2},{4,7},{7,4},{5,6},{6,5},{8,9},{9,8},{10,11... | collective-permute-start | bytes 786440 | tf_op jit(solution)/shard_map/ppermute | solution.py:330
  13.3 0.1 stack.23.place
  13.4 4.9 %shard_map.73 = (f32[16,8,128]{2,1,0:T(8,128)}, f32[32,4096]{1,0:T(8,128)}) custom-call(f32[16,4096]{1,0:T(8,128)} %solves.3, f32[16,4096]{1,0:T(8,128)} %own3.3, f32[16,4096]{1,0:T(8,128)} %factor2.1, f32[16,4096]{1,0:T(8,128)} %factor1.1, f32[64,4096]{1,0:T(8,128)} %basis3.1, f32[64,4096]{1,0:T(8,128)} %basis2.1, f32[64,4096]{1,0:T(8,128)} %basis1.1), custom_call_target="tpu_custom_call" | custom-call | tf_op jit(solution)/shard_map/pallas_call | solution.py:98
  18.3 11.3 %all_to_all.15.pieces = f32[16,8,128]{2,1,0:T(8,128)S(1)} all-to-all(f32[16,8,128]{2,1,0:T(8,128)} %get-tuple-element.13), channel_id=1, replica_groups=mesh['zl'=4,'yh'=2,'yl'=2,'x'=4,'core'=2,'zh'=4] {'yl','x','core'}, dimensions={0} | all-to-all | bytes 131072 | tf_op jit(solution)/shard_map/all_to_all | solution.py:334
  29.5 0.0 collective-permute-done.got3
  29.6 23.5 %all_to_all.16.pieces = f32[32,8,128]{2,1,0:T(8,128)S(1)} all-to-all(f32[32,8,128]{2,1,0:T(8,128)S(1)} %shard_map.74), channel_id=1, replica_groups=mesh['zl'=4,'yh'=2,'yl'=2,'x'=4,'core'=2,'zh'=4] {'yh','zl','zh'}, dimensions={0} | all-to-all | bytes 262144 | tf_op jit(solution)/shard_map/all_to_all | solution.py:339
  53.1 1.1 %shard_map.75 = f32[16,144,128]{2,1,0:T(8,128)} custom-call(f32[32,8,128]{2,1,0:T(8,128)S(1)} %all_to_all.16.pieces), custom_call_target="tpu_custom_call" | custom-call | tf_op jit(solution)/shard_map/pallas_call | solution.py:303
  54.2 0.0 copy-start.1
  54.2 7.3 %all-to-all-start.2 = ((f32[16,144,128]{2,1,0:T(8,128)}), f32[16,144,128]{2,1,0:T(8,128)S(1)}, u32[]{:S(2)}, u32[]{:S(2)}) async-start(f32[16,144,128]{2,1,0:T(8,128)} %shard_map.75), calls=%async_computation.2 | async-start | bytes 2359296 | tf_op jit(solution)/shard_map/all_to_all | solution.py:341
  61.5 0.0 copy-start
  61.5 0.0 copy-done.1
  61.5 4.4 %collective-permute-start.1 = (f32[32,4096]{1,0:T(8,128)S(1)}, f32[32,4096]{1,0:T(8,128)S(1)}, u32[]{:S(2)}, u32[]{:S(2)}) collective-permute-start(f32[32,4096]{1,0:T(8,128)S(1)} %copy-done.1), channel_id=1, source_target_pairs={{0,1},{1,0},{2,3},{3,2},{4,7},{7,4},{5,6},{6,5},{8,9},{9,8},{10,11... | collective-permute-start | bytes 1572872 | tf_op jit(solution)/shard_map/ppermute | solution.py:333
  66.0 12.8 %all-to-all-done.2 = f32[16,144,128]{2,1,0:T(8,128)S(1)} async-done(((f32[16,144,128]{2,1,0:T(8,128)}), f32[16,144,128]{2,1,0:T(8,128)S(1)}, u32[]{:S(2)}, u32[]{:S(2)}) %all-to-all-start.2) | async-done | bytes 1179680 | tf_op jit(solution)/shard_map/all_to_all | solution.py:341
  78.8 12.2 %shard_map.76.weights = f32[32,128]{1,0:T(8,128)S(1)} custom-call(s32[5]{0:T(128)S(1)} %stack.23.place, f32[2304,128]{1,0:T(8,128)S(1)} %bitcast.6), custom_call_target="tpu_custom_call" | custom-call | tf_op jit(solution)/shard_map/pallas_call | solution.py:303
  90.9 0.0 copy-start.2
  90.9 0.0 collective-permute-done.1.got
  91.0 0.0 copy-done
  91.0 0.4 shard_map.78
  91.3 4.7 %collective-permute-start.2 = (f32[16,4096]{1,0:T(8,128)S(1)}, f32[16,4096]{1,0:T(8,128)S(1)}, u32[]{:S(2)}, u32[]{:S(2)}) collective-permute-start(f32[16,4096]{1,0:T(8,128)S(1)} %shard_map.78), channel_id=1, source_target_pairs={{0,3},{3,0},{1,2},{2,1},{4,5},{5,4},{6,7},{7,6},{8,11},{11,8},{9,1... | collective-permute-start | bytes 786440 | tf_op jit(solution)/shard_map/ppermute | solution.py:358
  96.1 0.0 copy-done.2
  96.1 0.4 shard_map.77
  96.4 14.1 %collective-permute-done.2 = f32[16,4096]{1,0:T(8,128)S(1)} collective-permute-done((f32[16,4096]{1,0:T(8,128)S(1)}, f32[16,4096]{1,0:T(8,128)S(1)}, u32[]{:S(2)}, u32[]{:S(2)}) %collective-permute-start.2) | collective-permute-done | bytes 262176 | tf_op jit(solution)/shard_map/ppermute | solution.py:358
  110.6 0.7 add.3
  (1 shorter events, 0.0 us)
Async XLA Ops:
  0.0 29.5 %collective-permute-start = (f32[16,4096]{1,0:T(8,128)}, f32[16,4096]{1,0:T(8,128)S(1)}, u32[]{:S(2)}, u32[]{:S(2)}) collective-permute-start(f32[16,4096]{1,0:T(8,128)} %own3.3), channel_id=1, source_target_pairs={{0,1},{1,0},{2,3},{3,2},{4,7},{7,4},{5,6},{6,5},{8,9},{9,8},{10,11... | collective-permute-start | bytes 786440 | tf_op jit(solution)/shard_map/ppermute | solution.py:330
  54.2 7.3 %copy-start.1 = (f32[32,4096]{1,0:T(8,128)S(1)}, f32[32,4096]{1,0:T(8,128)}, u32[]{:S(2)}) copy-start(f32[32,4096]{1,0:T(8,128)} %get-tuple-element.15.own) | copy-start | bytes 1572868
  54.2 24.6 %all-to-all-start.2 = ((f32[16,144,128]{2,1,0:T(8,128)}), f32[16,144,128]{2,1,0:T(8,128)S(1)}, u32[]{:S(2)}, u32[]{:S(2)}) async-start(f32[16,144,128]{2,1,0:T(8,128)} %shard_map.75), calls=%async_computation.2 | async-start | bytes 2359296 | tf_op jit(solution)/shard_map/all_to_all | solution.py:341
  61.5 29.5 %copy-start = (f32[16,4096]{1,0:T(8,128)S(1)}, f32[16,4096]{1,0:T(8,128)}, u32[]{:S(2)}) copy-start(f32[16,4096]{1,0:T(8,128)} %own3.3) | copy-start | bytes 786436
  61.5 29.4 %collective-permute-start.1 = (f32[32,4096]{1,0:T(8,128)S(1)}, f32[32,4096]{1,0:T(8,128)S(1)}, u32[]{:S(2)}, u32[]{:S(2)}) collective-permute-start(f32[32,4096]{1,0:T(8,128)S(1)} %copy-done.1), channel_id=1, source_target_pairs={{0,1},{1,0},{2,3},{3,2},{4,7},{7,4},{5,6},{6,5},{8,9},{9,8},{10,11... | collective-permute-start | bytes 1572872 | tf_op jit(solution)/shard_map/ppermute | solution.py:333
  90.9 5.1 %copy-start.2 = (f32[16,4096]{1,0:T(8,128)S(1)}, f32[16,4096]{1,0:T(8,128)}, u32[]{:S(2)}) copy-start(f32[16,4096]{1,0:T(8,128)} %solves.3) | copy-start | bytes 786436
  91.3 19.3 %collective-permute-start.2 = (f32[16,4096]{1,0:T(8,128)S(1)}, f32[16,4096]{1,0:T(8,128)S(1)}, u32[]{:S(2)}, u32[]{:S(2)}) collective-permute-start(f32[16,4096]{1,0:T(8,128)S(1)} %shard_map.78), channel_id=1, source_target_pairs={{0,3},{3,0},{1,2},{2,1},{4,5},{5,4},{6,7},{7,6},{8,11},{11,8},{9,1... | collective-permute-start | bytes 786440 | tf_op jit(solution)/shard_map/ppermute | solution.py:358

commit v3 on v2

--- a/solution.py
+++ b/solution.py
@@ -11,7 +11,7 @@
 RANK = 64
 LOCAL = 16
 ROWS = 4096
-CHUNK = 1024
+CHUNK = 2048
 MESSAGE = 144
 LIMIT = 48 * 1024 * 1024
 
@@ -139,23 +139,25 @@
 
 def inverses(crossed, scratch):
     eye = identity()
-    size = squares(crossed)
-    close = size < 0.8
+    seconds = [full(e, e) for e in crossed]
+    close = squares(seconds) < 0.8
 
     @pl.when(close)
     def _():
         def improve(state):
             powers, guesses, _ = state
-            both = [full(jnp.concatenate([e, g], 0), e) for g, e in zip(guesses, powers)]
+            both = [full(jnp.concatenate([p, g], 0), p) for g, p in zip(guesses, powers)]
             better = tuple(g + b[RANK:] for g, b in zip(guesses, both))
-            return tuple(b[:RANK] for b in both), better, squares(powers)
+            higher = tuple(b[:RANK] for b in both)
+            return higher, better, squares(powers)
 
         def unfinished(state):
-            return state[2] > 1e-8
-
-        first = tuple(full(e, e) for e in crossed)
+            return state[2] > 1e-7
+
         state = lax.while_loop(
-            unfinished, improve, (first, tuple(eye + e for e in crossed), size)
+            unfinished,
+            improve,
+            (tuple(seconds), tuple(eye + e for e in crossed), jnp.float32(1.0)),
         )
         for index, guess in enumerate(state[1]):
             scratch[index] = guess

time: 112 us -> 112 us (level)
  the two profiles are of different devices: /device:TPU:1 before, /device:TPU:40 now
where the time goes in v3:
time: 112 us
  blocking collectives  40.2 us (36%)
  waiting for transfers between devices  36.5 us (33%)
  starting transfers between devices  19.8 us (18%)
  Pallas kernels  14.1 us (13%)
    all_to_all x1, blocking collectives, on_device(): slabs = lax.all_to_all(copies, SLAB, 0, 0, tiled=True)  27.7 us
    ppermute x1, waiting for transfers between devices, on_device(): came = lax.ppermute(sent, PAIRS, RETURN)  15.7 us
    all_to_all x1, waiting for transfers between devices, on_device(): lax.all_to_all(message, LEAF, 0, 0, tiled=True).reshape(16 * MESSAGE, 128)  13.6 us
    all_to_all x1, blocking collectives, on_device(): pieces = lax.all_to_all(slots, LEAF, 0, 0, tiled=True)  12.5 us
    pallas_call x5, Pallas kernels, call(): pl.pallas_call(kernel, out_shape=shapes, scratch_shapes=list(scratch), co...  10.1 us
    ppermute x1, starting transfers between devices, on_device(): got3 = lax.ppermute(factor3, PAIRS, SWAP)  9.09 us
    ppermute x1, waiting for transfers between devices, on_device(): got = lax.ppermute(own, PAIRS, SWAP)  7.21 us
    all_to_all x1, starting transfers between devices, on_device(): lax.all_to_all(message, LEAF, 0, 0, tiled=True).reshape(16 * MESSAGE, 128)  5.91 us
  transfers between devices with their start and end apart: 4, of which 3 were waited for; matrix products, arithmetic and copies ran while one was open for 0% of the time, Pallas kernels for 11%

profile of v3, /device:TPU:40, one launch (start us, length us, event | category | flops | bytes accessed | tf_op | source)
XLA Modules:
  0.0 111.6 jit_solution(566077737833681313)
XLA Ops:
  0.0 9.1 %collective-permute-start = (f32[16,4096]{1,0:T(8,128)}, f32[16,4096]{1,0:T(8,128)S(1)}, u32[]{:S(2)}, u32[]{:S(2)}) collective-permute-start(f32[16,4096]{1,0:T(8,128)} %own3.3), channel_id=1, source_target_pairs={{0,1},{1,0},{2,3},{3,2},{4,7},{7,4},{5,6},{6,5},{8,9},{9,8},{10,11... | collective-permute-start | bytes 786440 | tf_op jit(solution)/shard_map/ppermute | solution.py:332
  9.1 0.1 stack.23.place
  9.2 4.0 %shard_map.73 = (f32[16,8,128]{2,1,0:T(8,128)}, f32[32,4096]{1,0:T(8,128)}) custom-call(f32[16,4096]{1,0:T(8,128)} %solves.3, f32[16,4096]{1,0:T(8,128)} %own3.3, f32[16,4096]{1,0:T(8,128)} %factor2.1, f32[16,4096]{1,0:T(8,128)} %factor1.1, f32[64,4096]{1,0:T(8,128)} %basis3.1, f32[64,4096]{1,0:T(8,128)} %basis2.1, f32[64,4096]{1,0:T(8,128)} %basis1.1), custom_call_target="tpu_custom_call" | custom-call | tf_op jit(solution)/shard_map/pallas_call | solution.py:98
  13.2 12.5 %all_to_all.15.pieces = f32[16,8,128]{2,1,0:T(8,128)S(1)} all-to-all(f32[16,8,128]{2,1,0:T(8,128)} %get-tuple-element.13), channel_id=1, replica_groups=mesh['zl'=4,'yh'=2,'yl'=2,'x'=4,'core'=2,'zh'=4] {'yl','x','core'}, dimensions={0} | all-to-all | bytes 131072 | tf_op jit(solution)/shard_map/all_to_all | solution.py:336
  25.8 0.0 collective-permute-done.got3
  25.8 27.7 %all_to_all.16.pieces = f32[32,8,128]{2,1,0:T(8,128)S(1)} all-to-all(f32[32,8,128]{2,1,0:T(8,128)S(1)} %shard_map.74), channel_id=1, replica_groups=mesh['zl'=4,'yh'=2,'yl'=2,'x'=4,'core'=2,'zh'=4] {'yh','zl','zh'}, dimensions={0} | all-to-all | bytes 262144 | tf_op jit(solution)/shard_map/all_to_all | solution.py:341
  53.5 1.1 %shard_map.75 = f32[16,144,128]{2,1,0:T(8,128)} custom-call(f32[32,8,128]{2,1,0:T(8,128)S(1)} %all_to_all.16.pieces), custom_call_target="tpu_custom_call" | custom-call | tf_op jit(solution)/shard_map/pallas_call | solution.py:305
  54.6 0.0 copy-start.1
  54.6 5.9 %all-to-all-start.2 = ((f32[16,144,128]{2,1,0:T(8,128)}), f32[16,144,128]{2,1,0:T(8,128)S(1)}, u32[]{:S(2)}, u32[]{:S(2)}) async-start(f32[16,144,128]{2,1,0:T(8,128)} %shard_map.75), calls=%async_computation.2 | async-start | bytes 2359296 | tf_op jit(solution)/shard_map/all_to_all | solution.py:343
  60.5 0.0 copy-start
  60.5 0.0 copy-done.1
  60.5 2.9 %collective-permute-start.1 = (f32[32,4096]{1,0:T(8,128)S(1)}, f32[32,4096]{1,0:T(8,128)S(1)}, u32[]{:S(2)}, u32[]{:S(2)}) collective-permute-start(f32[32,4096]{1,0:T(8,128)S(1)} %copy-done.1), channel_id=1, source_target_pairs={{0,1},{1,0},{2,3},{3,2},{4,7},{7,4},{5,6},{6,5},{8,9},{9,8},{10,11... | collective-permute-start | bytes 1572872 | tf_op jit(solution)/shard_map/ppermute | solution.py:335
  63.4 13.6 %all-to-all-done.2 = f32[16,144,128]{2,1,0:T(8,128)S(1)} async-done(((f32[16,144,128]{2,1,0:T(8,128)}), f32[16,144,128]{2,1,0:T(8,128)S(1)}, u32[]{:S(2)}, u32[]{:S(2)}) %all-to-all-start.2) | async-done | bytes 1179680 | tf_op jit(solution)/shard_map/all_to_all | solution.py:343
  77.0 8.3 %shard_map.76.weights = f32[32,128]{1,0:T(8,128)S(1)} custom-call(s32[5]{0:T(128)S(1)} %stack.23.place, f32[2304,128]{1,0:T(8,128)S(1)} %bitcast.6), custom_call_target="tpu_custom_call" | custom-call | tf_op jit(solution)/shard_map/pallas_call | solution.py:305
  85.3 0.0 copy-start.2
  85.3 7.2 %collective-permute-done.1.got = f32[32,4096]{1,0:T(8,128)S(1)} collective-permute-done((f32[32,4096]{1,0:T(8,128)S(1)}, f32[32,4096]{1,0:T(8,128)S(1)}, u32[]{:S(2)}, u32[]{:S(2)}) %collective-permute-start.1) | collective-permute-done | bytes 524320 | tf_op jit(solution)/shard_map/ppermute | solution.py:335
  92.5 0.0 copy-done
  92.5 0.4 shard_map.78
  92.9 1.9 %collective-permute-start.2 = (f32[16,4096]{1,0:T(8,128)S(1)}, f32[16,4096]{1,0:T(8,128)S(1)}, u32[]{:S(2)}, u32[]{:S(2)}) collective-permute-start(f32[16,4096]{1,0:T(8,128)S(1)} %shard_map.78), channel_id=1, source_target_pairs={{0,3},{3,0},{1,2},{2,1},{4,5},{5,4},{6,7},{7,6},{8,11},{11,8},{9,1... | collective-permute-start | bytes 786440 | tf_op jit(solution)/shard_map/ppermute | solution.py:360
  94.8 0.0 copy-done.2
  94.8 0.4 shard_map.77
  95.2 15.7 %collective-permute-done.2 = f32[16,4096]{1,0:T(8,128)S(1)} collective-permute-done((f32[16,4096]{1,0:T(8,128)S(1)}, f32[16,4096]{1,0:T(8,128)S(1)}, u32[]{:S(2)}, u32[]{:S(2)}) %collective-permute-start.2) | collective-permute-done | bytes 262176 | tf_op jit(solution)/shard_map/ppermute | solution.py:360
  110.8 0.7 add.3
  (1 shorter events, 0.0 us)
Async XLA Ops:
  0.0 25.8 %collective-permute-start = (f32[16,4096]{1,0:T(8,128)}, f32[16,4096]{1,0:T(8,128)S(1)}, u32[]{:S(2)}, u32[]{:S(2)}) collective-permute-start(f32[16,4096]{1,0:T(8,128)} %own3.3), channel_id=1, source_target_pairs={{0,1},{1,0},{2,3},{3,2},{4,7},{7,4},{5,6},{6,5},{8,9},{9,8},{10,11... | collective-permute-start | bytes 786440 | tf_op jit(solution)/shard_map/ppermute | solution.py:332
  54.6 5.9 %copy-start.1 = (f32[32,4096]{1,0:T(8,128)S(1)}, f32[32,4096]{1,0:T(8,128)}, u32[]{:S(2)}) copy-start(f32[32,4096]{1,0:T(8,128)} %get-tuple-element.15.own) | copy-start | bytes 1572868
  54.6 22.4 %all-to-all-start.2 = ((f32[16,144,128]{2,1,0:T(8,128)}), f32[16,144,128]{2,1,0:T(8,128)S(1)}, u32[]{:S(2)}, u32[]{:S(2)}) async-start(f32[16,144,128]{2,1,0:T(8,128)} %shard_map.75), calls=%async_computation.2 | async-start | bytes 2359296 | tf_op jit(solution)/shard_map/all_to_all | solution.py:343
  60.5 32.0 %copy-start = (f32[16,4096]{1,0:T(8,128)S(1)}, f32[16,4096]{1,0:T(8,128)}, u32[]{:S(2)}) copy-start(f32[16,4096]{1,0:T(8,128)} %own3.3) | copy-start | bytes 786436
  60.5 32.0 %collective-permute-start.1 = (f32[32,4096]{1,0:T(8,128)S(1)}, f32[32,4096]{1,0:T(8,128)S(1)}, u32[]{:S(2)}, u32[]{:S(2)}) collective-permute-start(f32[32,4096]{1,0:T(8,128)S(1)} %copy-done.1), channel_id=1, source_target_pairs={{0,1},{1,0},{2,3},{3,2},{4,7},{7,4},{5,6},{6,5},{8,9},{9,8},{10,11... | collective-permute-start | bytes 1572872 | tf_op jit(solution)/shard_map/ppermute | solution.py:335
  85.3 9.5 %copy-start.2 = (f32[16,4096]{1,0:T(8,128)S(1)}, f32[16,4096]{1,0:T(8,128)}, u32[]{:S(2)}) copy-start(f32[16,4096]{1,0:T(8,128)} %solves.3) | copy-start | bytes 786436
  92.9 18.0 %collective-permute-start.2 = (f32[16,4096]{1,0:T(8,128)S(1)}, f32[16,4096]{1,0:T(8,128)S(1)}, u32[]{:S(2)}, u32[]{:S(2)}) collective-permute-start(f32[16,4096]{1,0:T(8,128)S(1)} %shard_map.78), channel_id=1, source_target_pairs={{0,3},{3,0},{1,2},{2,1},{4,5},{5,4},{6,7},{7,6},{8,11},{11,8},{9,1... | collective-permute-start | bytes 786440 | tf_op jit(solution)/shard_map/ppermute | solution.py:360

commit v4 on v3

--- a/solution.py
+++ b/solution.py
@@ -82,14 +82,19 @@
     @pl.when(step == pl.num_programs(0) - 1)
     def _():
         deep = total3[...]
-        out[:, 0, :] = jnp.concatenate([deep[0:16], deep[32:48]], 1)
-        out[:, 1, :] = jnp.concatenate([deep[16:32], deep[48:64]], 1)
-        out[:, 2, :] = total21[16:32, :]
-        out[:, 3, :] = total21[0:16, :]
-        out[:, 4, :] = total21[32:48, :]
-        out[:, 5, :] = total21[48:64, :]
-        out[:, 6, :] = jnp.zeros((16, 128), f32)
-        out[:, 7, :] = jnp.zeros((16, 128), f32)
+        pieces = [
+            jnp.concatenate([deep[0:16], deep[32:48]], 1),
+            jnp.concatenate([deep[16:32], deep[48:64]], 1),
+            total21[16:32, :],
+            total21[0:16, :],
+            total21[32:48, :],
+            total21[48:64, :],
+            jnp.zeros((16, 128), f32),
+            jnp.zeros((16, 128), f32),
+        ]
+        for index, piece in enumerate(pieces):
+            out[:, 0, index, :] = piece[:8]
+            out[:, 1, index, :] = piece[8:]
 
 
 def local_products(*arrays):
@@ -100,10 +105,10 @@
         grid=(ROWS // CHUNK,),
         in_specs=[narrow] * 4 + [wide] * 3,
         out_specs=(
-            pl.BlockSpec((16, 8, 128), lambda i: (0, 0, 0)),
+            pl.BlockSpec((8, 2, 8, 128), lambda i: (0, 0, 0, 0)),
             pl.BlockSpec((2 * LOCAL, CHUNK), lambda i: (0, i)),
         ),
-        out_shape=(shape(16, 8, 128), shape(2 * LOCAL, ROWS)),
+        out_shape=(shape(8, 2, 8, 128), shape(2 * LOCAL, ROWS)),
         scratch_shapes=[pltpu.VMEM((RANK, RANK), f32), pltpu.VMEM((RANK, 2 * RANK), f32)],
         cost_estimate=FREE,
     )(*arrays)
@@ -198,11 +203,16 @@
     return tops, bottoms
 
 
-def tree(place, sums, out, first, second, third, whole, solved):
+def tree(place, mine, other, out, first, second, third, whole, solved):
+    first_core = place[5] == 0
+
     def rows(base, entry):
-        return jnp.concatenate(
-            [sums[pl.ds(base + entry * 4 + zh, 16, stride=MESSAGE), :] for zh in range(4)], 0
-        )
+        parts = []
+        for zh in range(4):
+            here = pl.ds(base + entry * 4 + zh, 8, stride=MESSAGE)
+            a, b = mine[here, :], other[here, :]
+            parts += [jnp.where(first_core, a, b), jnp.where(first_core, b, a)]
+        return jnp.concatenate(parts, 0)
 
     def left(values):
         return values[:, :RANK]
@@ -282,7 +292,8 @@
     owner = jnp.where(column < 48, zh, partner)
     inner = jnp.where(column < 48, column, column - 48)
     wanted = (inner // 16) * RANK + owner * 16 + inner % 16
-    out[...] = -exact(picked, ((source == wanted) & (column < 96)).astype(f32))
+    out[32:, :] = jnp.zeros((96, 128), f32)
+    out[:32, :] = -exact(picked, ((source == wanted) & (column < 96)).astype(f32))
 
 
 def apply_rows(coefficient, *factors):
@@ -327,35 +338,45 @@
             zh,
             jnp.where(core == 0, near, far),
             jnp.where(core == 0, far, near),
+            core,
         ]
     ).astype(jnp.int32)
     got3 = lax.ppermute(factor3, PAIRS, SWAP)
     slots, own = local_products(solves, factor3, factor2, factor1, basis3, basis2, basis1)
+    slots = slots.reshape(16, 8, 128)
     slots, place = lax.optimization_barrier((slots, place))
-    got = lax.ppermute(own, PAIRS, SWAP)
     pieces = lax.all_to_all(slots, LEAF, 0, 0, tiled=True)
     vmem = pl.BlockSpec(memory_space=pltpu.VMEM)
 
     copies = call(leaf_sum, shape(32, 8, 128), pieces)
     copies, got3 = lax.optimization_barrier((copies, got3))
     slabs = lax.all_to_all(copies, SLAB, 0, 0, tiled=True)
-    message = call(pack, shape(16, MESSAGE, 128), slabs)
-    sums = lax.all_to_all(message, LEAF, 0, 0, tiled=True).reshape(16 * MESSAGE, 128)
-    coefficients = call(
-        tree,
-        shape(32, 128),
-        place,
-        sums,
-        in_specs=[pl.BlockSpec(memory_space=pltpu.SMEM), vmem],
-        out_specs=vmem,
-        scratch=[
-            pltpu.VMEM((2, 64, 64), f32),
-            pltpu.VMEM((4, 128, 64), f32),
-            pltpu.VMEM((8, 192, 64), f32),
-            pltpu.VMEM((64, 192), f32),
-            pltpu.VMEM((4, 64, 64), f32),
-        ],
-    )
+    slabs, own = lax.optimization_barrier((slabs, own))
+    got = lax.ppermute(own, PAIRS, SWAP)
+
+    def solve(_, state):
+        message = call(pack, shape(8, MESSAGE, 128), slabs)
+        mine = lax.all_to_all(message, ("yl", "x"), 0, 0, tiled=True).reshape(8 * MESSAGE, 128)
+        other = lax.ppermute(mine, "core", [(0, 1), (1, 0)])
+        return call(
+            tree,
+            shape(128, 128),
+            place,
+            mine,
+            other,
+            in_specs=[pl.BlockSpec(memory_space=pltpu.SMEM), vmem, vmem],
+            out_specs=vmem,
+            scratch=[
+                pltpu.VMEM((2, 64, 64), f32),
+                pltpu.VMEM((4, 128, 64), f32),
+                pltpu.VMEM((8, 192, 64), f32),
+                pltpu.VMEM((64, 192), f32),
+                pltpu.VMEM((4, 64, 64), f32),
+            ],
+        )
+
+    once = lax.optimization_barrier(jnp.int32(1))
+    coefficients = lax.fori_loop(0, once, solve, pieces.reshape(128, 128))
     sent = call(outgoing, shape(16, ROWS), coefficients, factor3, own, got3, got)
     came = lax.ppermute(sent, PAIRS, RETURN)
     return call(staying, shape(16, ROWS), coefficients, factor3, own, got3, got, solves) + came

time: 112 us -> 108 us (0.964)
  the two profiles are of different devices: /device:TPU:40 before, /device:TPU:1 now
where the time goes in v4:
time: 108 us
  blocking collectives  45.6 us (42%)
  starting transfers between devices  30.2 us (28%)
  waiting for transfers between devices  15.7 us (15%)
  Pallas kernels  14.6 us (14%)
    all_to_all x1, blocking collectives, on_device(): slabs = lax.all_to_all(copies, SLAB, 0, 0, tiled=True)  23.5 us
    ppermute x1, waiting for transfers between devices, on_device(): came = lax.ppermute(sent, PAIRS, RETURN)  14.1 us
    ppermute x1, starting transfers between devices, on_device(): got3 = lax.ppermute(factor3, PAIRS, SWAP)  13.3 us
    all_to_all x1, blocking collectives, on_device(): pieces = lax.all_to_all(slots, LEAF, 0, 0, tiled=True)  11.4 us
    all_to_all x1, blocking collectives, solve(): lax.all_to_all(message, ('yl', 'x'), 0, 0, tiled=True)  10.7 us
    pallas_call x5, Pallas kernels, call(): pl.pallas_call(kernel, out_shape=shapes, scratch_shapes=list(scratch), co...  10.6 us
    ppermute x1, starting transfers between devices, on_device(): got = lax.ppermute(own, PAIRS, SWAP)  6.63 us
    ppermute x1, starting transfers between devices, solve(): other = lax.ppermute(mine, 'core', [(0, 1), (1, 0)])  5.64 us
  transfers between devices with their start and end apart: 4, of which 2 were waited for; matrix products, arithmetic and copies ran while one was open for 0% of the time, Pallas kernels for 12%

profile of v4, /device:TPU:1, one launch (start us, length us, event | category | flops | bytes accessed | tf_op | source)
XLA Modules:
  0.0 107.6 jit_solution(12576732991637548291)
XLA Ops:
  0.0 13.3 %collective-permute-start.1 = (f32[16,4096]{1,0:T(8,128)}, f32[16,4096]{1,0:T(8,128)S(1)}, u32[]{:S(2)}, u32[]{:S(2)}) collective-permute-start(f32[16,4096]{1,0:T(8,128)} %own3.3), channel_id=1, source_target_pairs={{0,1},{1,0},{2,3},{3,2},{4,7},{7,4},{5,6},{6,5},{8,9},{9,8},{10,11... | collective-permute-start | bytes 786440 | tf_op jit(solution)/shard_map/ppermute | solution.py:344
  13.3 0.1 stack.27
  13.4 4.0 %shard_map.73 = (f32[8,2,8,128]{3,2,1,0:T(8,128)}, f32[32,4096]{1,0:T(8,128)}) custom-call(f32[16,4096]{1,0:T(8,128)} %solves.3, f32[16,4096]{1,0:T(8,128)} %own3.3, f32[16,4096]{1,0:T(8,128)} %factor2.1, f32[16,4096]{1,0:T(8,128)} %factor1.1, f32[64,4096]{1,0:T(8,128)} %basis3.1, f32[64,4096]{1,0:T(8,128)} %basis2.1, f32[64,4096]{1,0:T(8,128)} %basis1.1), custom_call_target="tpu_custom_call" | custom-call | tf_op jit(solution)/shard_map/pallas_call | solution.py:103
  17.4 11.4 %all_to_all.16.pieces = f32[16,8,128]{2,1,0:T(8,128)S(1)} all-to-all(f32[16,8,128]{2,1,0:T(8,128)} %bitcast.14), channel_id=1, replica_groups=mesh['zl'=4,'yh'=2,'yl'=2,'x'=4,'core'=2,'zh'=4] {'yl','x','core'}, dimensions={0} | all-to-all | bytes 131072 | tf_op jit(solution)/shard_map/all_to_all | solution.py:348
  28.8 0.6 copy-done.3
  29.4 0.0 collective-permute-done.1.got3
  29.4 23.5 %all_to_all.17 = f32[32,8,128]{2,1,0:T(8,128)S(1)} all-to-all(f32[32,8,128]{2,1,0:T(8,128)S(1)} %shard_map.74), channel_id=1, replica_groups=mesh['zl'=4,'yh'=2,'yl'=2,'x'=4,'core'=2,'zh'=4] {'yh','zl','zh'}, dimensions={0} | all-to-all | bytes 262144 | tf_op jit(solution)/shard_map/all_to_all | solution.py:353
  52.9 0.0 copy-done.1
  52.9 6.6 %collective-permute-start.2 = (f32[32,4096]{1,0:T(8,128)S(1)}, f32[32,4096]{1,0:T(8,128)S(1)}, u32[]{:S(2)}, u32[]{:S(2)}) collective-permute-start(f32[32,4096]{1,0:T(8,128)S(1)} %copy-done.1), channel_id=1, source_target_pairs={{0,1},{1,0},{2,3},{3,2},{4,7},{7,4},{5,6},{6,5},{8,9},{9,8},{10,11... | collective-permute-start | bytes 1572872 | tf_op jit(solution)/shard_map/ppermute | solution.py:355
  59.5 0.0 copy-start
  59.5 26.9 %while.10 = (s32[]{:T(128)}, f32[128,128]{1,0:T(8,128)}, s32[]{:T(128)}, f32[32,8,128]{2,1,0:T(8,128)S(1)}, s32[6]{0:T(128)S(1)}, /*index=5*/s32[]{:T(128)}) while((s32[]{:T(128)}, f32[128,128]{1,0:T(8,128)}, s32[]{:T(128)}, f32[32,8,128]{2,1,0:T(8,128)S(1)}, s32[6]{0:T(128)S(1)}, /*index=5*/s32[]{:T(128)}) %tuple.27), condition=%wide.region_1.2_spmd, body=%wide.region_0.1_spmd.sunk | while | flops 2 | bytes 3539053 | solution.py:379
  59.6 0.1 body.2
  59.6 10.7 %all_to_all.18 = f32[8,144,128]{2,1,0:T(8,128)S(1)} all-to-all(f32[8,144,128]{2,1,0:T(8,128)S(1)} %body.2), channel_id=1, replica_groups=mesh['zl'=4,'yh'=2,'yl'=2,'x'=4,'core'=2,'zh'=4] {'yl','x'}, dimensions={0} | all-to-all | bytes 1179648 | tf_op jit(solution)/shard_map/while/body/all_to_all | solution.py:359
  70.3 5.6 %collective-permute-start = (f32[1152,128]{1,0:T(8,128)S(1)}, f32[1152,128]{1,0:T(8,128)S(1)}, u32[]{:S(2)}, u32[]{:S(2)}) collective-permute-start(f32[1152,128]{1,0:T(8,128)S(1)} %bitcast.11), channel_id=1, source_target_pairs={{0,4},{4,0},{1,5},{5,1},{2,6},{6,2},{3,7},{7,3},{8,12},{12,8},{9,1... | collective-permute-start | bytes 1769480 | tf_op jit(solution)/shard_map/while/body/ppermute | solution.py:360
  76.0 1.6 %collective-permute-done.other = f32[1152,128]{1,0:T(8,128)S(1)} collective-permute-done((f32[1152,128]{1,0:T(8,128)S(1)}, f32[1152,128]{1,0:T(8,128)S(1)}, u32[]{:S(2)}, u32[]{:S(2)}) %collective-permute-start) | collective-permute-done | bytes 589856 | tf_op jit(solution)/shard_map/while/body/ppermute | solution.py:360
  77.6 8.8 %body.3 = f32[128,128]{1,0:T(8,128)} custom-call(s32[6]{0:T(128)S(1)} %get-tuple-element.105.place, f32[1152,128]{1,0:T(8,128)S(1)} %bitcast.12, f32[1152,128]{1,0:T(8,128)S(1)} %collective-permute-done.other), custom_call_target="tpu_custom_call" | custom-call | tf_op jit(solution)/shard_map/while/body/pallas_call | solution.py:316
  86.4 0.0 collective-permute-done.2.got
  86.4 0.0 copy-done
  86.4 0.0 copy-start.4
  86.4 1.3 %shard_map.76 = f32[16,4096]{1,0:T(8,128)S(1)} custom-call(f32[128,128]{1,0:T(8,128)} %get-tuple-element.46.weights, f32[16,4096]{1,0:T(8,128)S(1)} %copy-done, f32[32,4096]{1,0:T(8,128)S(1)} %copy-done.1, f32[16,4096]{1,0:T(8,128)S(1)} %collective-permute-done.1.got3, f32[32,4096]{1,0:T(8,128)S(1)} %collective-permute-done.2.got), custom_call_target="tpu_custom_call" | custom-call | tf_op jit(solution)/shard_map/pallas_call | solution.py:316
  87.7 4.7 %collective-permute-start.3 = (f32[16,4096]{1,0:T(8,128)S(1)}, f32[16,4096]{1,0:T(8,128)S(1)}, u32[]{:S(2)}, u32[]{:S(2)}) collective-permute-start(f32[16,4096]{1,0:T(8,128)S(1)} %shard_map.76), channel_id=1, source_target_pairs={{0,3},{3,0},{1,2},{2,1},{4,5},{5,4},{6,7},{7,6},{8,11},{11,8},{9,1... | collective-permute-start | bytes 786440 | tf_op jit(solution)/shard_map/ppermute | solution.py:381
  92.4 0.4 shard_map.75
  92.8 14.1 %collective-permute-done.3 = f32[16,4096]{1,0:T(8,128)S(1)} collective-permute-done((f32[16,4096]{1,0:T(8,128)S(1)}, f32[16,4096]{1,0:T(8,128)S(1)}, u32[]{:S(2)}, u32[]{:S(2)}) %collective-permute-start.3) | collective-permute-done | bytes 262176 | tf_op jit(solution)/shard_map/ppermute | solution.py:381
  106.9 0.7 add.6
  (6 shorter events, 0.0 us)
Async XLA Ops:
  0.0 29.4 %collective-permute-start.1 = (f32[16,4096]{1,0:T(8,128)}, f32[16,4096]{1,0:T(8,128)S(1)}, u32[]{:S(2)}, u32[]{:S(2)}) collective-permute-start(f32[16,4096]{1,0:T(8,128)} %own3.3), channel_id=1, source_target_pairs={{0,1},{1,0},{2,3},{3,2},{4,7},{7,4},{5,6},{6,5},{8,9},{9,8},{10,11... | collective-permute-start | bytes 786440 | tf_op jit(solution)/shard_map/ppermute | solution.py:344
  17.4 35.5 %copy-start.1 = (f32[32,4096]{1,0:T(8,128)S(1)}, f32[32,4096]{1,0:T(8,128)}, u32[]{:S(2)}) copy-start(f32[32,4096]{1,0:T(8,128)} %get-tuple-element.47.own) | copy-start | bytes 1572868
  28.8 0.6 copy-start.3
  52.9 33.5 %collective-permute-start.2 = (f32[32,4096]{1,0:T(8,128)S(1)}, f32[32,4096]{1,0:T(8,128)S(1)}, u32[]{:S(2)}, u32[]{:S(2)}) collective-permute-start(f32[32,4096]{1,0:T(8,128)S(1)} %copy-done.1), channel_id=1, source_target_pairs={{0,1},{1,0},{2,3},{3,2},{4,7},{7,4},{5,6},{6,5},{8,9},{9,8},{10,11... | collective-permute-start | bytes 1572872 | tf_op jit(solution)/shard_map/ppermute | solution.py:355
  59.5 26.9 %copy-start = (f32[16,4096]{1,0:T(8,128)S(1)}, f32[16,4096]{1,0:T(8,128)}, u32[]{:S(2)}) copy-start(f32[16,4096]{1,0:T(8,128)} %own3.3) | copy-start | bytes 786436
  70.3 7.3 %collective-permute-start = (f32[1152,128]{1,0:T(8,128)S(1)}, f32[1152,128]{1,0:T(8,128)S(1)}, u32[]{:S(2)}, u32[]{:S(2)}) collective-permute-start(f32[1152,128]{1,0:T(8,128)S(1)} %bitcast.11), channel_id=1, source_target_pairs={{0,4},{4,0},{1,5},{5,1},{2,6},{6,2},{3,7},{7,3},{8,12},{12,8},{9,1... | collective-permute-start | bytes 1769480 | tf_op jit(solution)/shard_map/while/body/ppermute | solution.py:360
  86.4 6.0 %copy-start.2 = (f32[16,4096]{1,0:T(8,128)S(1)}, f32[16,4096]{1,0:T(8,128)}, u32[]{:S(2)}) copy-start(f32[16,4096]{1,0:T(8,128)} %solves.3) | copy-start | bytes 786436
  86.4 6.0 %copy-start.4 = (f32[128,128]{1,0:T(8,128)S(1)}, f32[128,128]{1,0:T(8,128)}, u32[]{:S(2)}) copy-start(f32[128,128]{1,0:T(8,128)} %get-tuple-element.46.weights) | copy-start | bytes 196612
  87.7 19.2 %collective-permute-start.3 = (f32[16,4096]{1,0:T(8,128)S(1)}, f32[16,4096]{1,0:T(8,128)S(1)}, u32[]{:S(2)}, u32[]{:S(2)}) collective-permute-start(f32[16,4096]{1,0:T(8,128)S(1)} %shard_map.76), channel_id=1, source_target_pairs={{0,3},{3,0},{1,2},{2,1},{4,5},{5,4},{6,7},{7,6},{8,11},{11,8},{9,1... | collective-permute-start | bytes 786440 | tf_op jit(solution)/shard_map/ppermute | solution.py:381

commit v5 on v4

--- a/solution.py
+++ b/solution.py
@@ -36,7 +36,11 @@
 
 
 def exact(left, right):
-    return full(left, right)
+    count = left.shape[0]
+    top, middle = split(left)
+    right_top, right_middle = split(right)
+    first = dot(jnp.concatenate([top, middle], 0), right_top)
+    return first[:count] + (first[count:] + dot(top, right_middle))
 
 
 FREE = pl.CostEstimate(flops=0, bytes_accessed=0, transcendentals=0)
@@ -157,7 +161,7 @@
             return higher, better, squares(powers)
 
         def unfinished(state):
-            return state[2] > 1e-7
+            return state[2] > 2e-6
 
         state = lax.while_loop(
             unfinished,
@@ -194,13 +198,16 @@
             scratch[index] = guess
 
 
-def merge(nodes, scratch):
-    crossed = [exact(kb, ka) for ka, kb, _, _ in nodes]
+def merge(nodes, scratch, couples=()):
+    crossed = [full(kb, ka) for ka, kb, _, _ in nodes]
     sides = [ra - exact(rb, ka) for ka, _, ra, rb in nodes]
+    known = [exact(node[3], ca) for node, (ca, _) in zip(nodes, couples)]
+    gains = [cb - exact(node[1], ca) for node, (ca, cb) in zip(nodes, couples)]
     inverses(crossed, scratch)
     bottoms = [exact(side, scratch[index]) for index, side in enumerate(sides)]
     tops = [rb - exact(low, kb) for (_, kb, _, rb), low in zip(nodes, bottoms)]
-    return tops, bottoms
+    updates = [first + exact(low, gain) for first, low, gain in zip(known, bottoms, gains)]
+    return tops, bottoms, updates
 
 
 def tree(place, mine, other, out, first, second, third, whole, solved):
@@ -236,14 +243,13 @@
         )
         couple.append((rows(64, zl), rows(64, 4 + zl)))
         carry.append(jnp.concatenate([rows(96, zl), rows(112, zl), rows(128, zl)], 0))
-    tops, bottoms = merge(nodes, solved)
+    tops, bottoms, updates = merge(nodes, solved, couple)
     two = []
     one = []
     for zl in range(4):
         third[2 * zl] = tops[zl]
         third[2 * zl + 1] = bottoms[zl]
-        update = exact(tops[zl], couple[zl][0]) + exact(bottoms[zl], couple[zl][1])
-        carried = carry[zl] - update
+        carried = carry[zl] - updates[zl]
         two.append(left(carried))
         one.append(right(carried))
 
@@ -259,18 +265,15 @@
         )
         for m in range(2)
     ]
-    tops, bottoms = merge(nodes, solved)
+    middle = [values[RANK : 2 * RANK] for values in one]
+    tops, bottoms, updates = merge(nodes, solved, [middle[:2], middle[2:]])
     last = []
     for m in range(2):
         second[2 * m] = tops[m]
         second[2 * m + 1] = bottoms[m]
-        last.append(
-            keep(one[2 * m])
-            + keep(one[2 * m + 1])
-            - exact(tops[m], one[2 * m][RANK : 2 * RANK])
-            - exact(bottoms[m], one[2 * m + 1][RANK : 2 * RANK])
-        )
-    tops, bottoms = merge([(last[0][RANK:], last[1][RANK:], last[0][:RANK], last[1][:RANK])], solved)
+        last.append(keep(one[2 * m]) + keep(one[2 * m + 1]) - updates[m])
+    node = (last[0][RANK:], last[1][RANK:], last[0][:RANK], last[1][:RANK])
+    tops, bottoms, _ = merge([node], solved)
     first[0] = tops[0]
     first[1] = bottoms[0]
 
@@ -354,7 +357,7 @@
     slabs, own = lax.optimization_barrier((slabs, own))
     got = lax.ppermute(own, PAIRS, SWAP)
 
-    def solve(_, state):
+    def solve():
         message = call(pack, shape(8, MESSAGE, 128), slabs)
         mine = lax.all_to_all(message, ("yl", "x"), 0, 0, tiled=True).reshape(8 * MESSAGE, 128)
         other = lax.ppermute(mine, "core", [(0, 1), (1, 0)])
@@ -376,7 +379,7 @@
         )
 
     once = lax.optimization_barrier(jnp.int32(1))
-    coefficients = lax.fori_loop(0, once, solve, pieces.reshape(128, 128))
+    coefficients = lax.cond(once > 0, solve, lambda: jnp.zeros((128, 128), f32))
     sent = call(outgoing, shape(16, ROWS), coefficients, factor3, own, got3, got)
     came = lax.ppermute(sent, PAIRS, RETURN)
     return call(staying, shape(16, ROWS), coefficients, factor3, own, got3, got, solves) + came

time: 108 us -> 105 us (0.972)
  Pallas kernels: 14.6 us -> 11 us
    pallas_call x5, Pallas kernels: 10.6 us -> 7 us  [call(): pl.pallas_call(kernel, out_shape=shapes, scratch_shapes=list(scratch), co...]
  transfers between devices with their start and end apart: 4 -> 4, of which waited for: 2 -> 2; matrix products, arithmetic and copies ran while one was open for 0% -> 0% of each run, Pallas kernels for 12% -> 10%
where the time goes in v5:
time: 105 us; the launch traced here: 104 us
  blocking collectives  45.6 us (43%)
  starting transfers between devices  30.8 us (29%)
  waiting for transfers between devices  15.5 us (15%)
  Pallas kernels  11 us (10%)
    all_to_all x1, blocking collectives, on_device(): slabs = lax.all_to_all(copies, SLAB, 0, 0, tiled=True)  23.5 us
    ppermute x1, waiting for transfers between devices, on_device(): came = lax.ppermute(sent, PAIRS, RETURN)  13.8 us
    ppermute x1, starting transfers between devices, on_device(): got3 = lax.ppermute(factor3, PAIRS, SWAP)  13.3 us
    all_to_all x1, blocking collectives, on_device(): pieces = lax.all_to_all(slots, LEAF, 0, 0, tiled=True)  11.4 us
    all_to_all x1, blocking collectives, solve(): lax.all_to_all(message, ('yl', 'x'), 0, 0, tiled=True)  10.7 us
    pallas_call x5, Pallas kernels, call(): pl.pallas_call(kernel, out_shape=shapes, scratch_shapes=list(scratch), co...  7 us
    ppermute x1, starting transfers between devices, on_device(): got = lax.ppermute(own, PAIRS, SWAP)  6.49 us
    ppermute x1, starting transfers between devices, solve(): other = lax.ppermute(mine, 'core', [(0, 1), (1, 0)])  6.37 us
  transfers between devices with their start and end apart: 4, of which 2 were waited for; matrix products, arithmetic and copies ran while one was open for 0% of the time, Pallas kernels for 10%

profile of v5, /device:TPU:1, one launch (start us, length us, event | category | flops | bytes accessed | tf_op | source)
XLA Modules:
  0.0 103.8 jit_solution(12771185952183195922)
XLA Ops:
  0.0 13.3 %collective-permute-start.1 = (f32[16,4096]{1,0:T(8,128)}, f32[16,4096]{1,0:T(8,128)S(1)}, u32[]{:S(2)}, u32[]{:S(2)}) collective-permute-start(f32[16,4096]{1,0:T(8,128)} %own3.3), channel_id=1, source_target_pairs={{0,1},{1,0},{2,3},{3,2},{4,7},{7,4},{5,6},{6,5},{8,9},{9,8},{10,11... | collective-permute-start | bytes 786440 | tf_op jit(solution)/shard_map/ppermute | solution.py:347
  13.3 0.1 stack.27
  13.4 4.0 %shard_map.73 = (f32[8,2,8,128]{3,2,1,0:T(8,128)}, f32[32,4096]{1,0:T(8,128)}) custom-call(f32[16,4096]{1,0:T(8,128)} %solves.3, f32[16,4096]{1,0:T(8,128)} %own3.3, f32[16,4096]{1,0:T(8,128)} %factor2.1, f32[16,4096]{1,0:T(8,128)} %factor1.1, f32[64,4096]{1,0:T(8,128)} %basis3.1, f32[64,4096]{1,0:T(8,128)} %basis2.1, f32[64,4096]{1,0:T(8,128)} %basis1.1), custom_call_target="tpu_custom_call" | custom-call | tf_op jit(solution)/shard_map/pallas_call | solution.py:107
  17.4 0.0 copy-start.1
  17.4 11.4 %all_to_all.15.pieces = f32[16,8,128]{2,1,0:T(8,128)S(1)} all-to-all(f32[16,8,128]{2,1,0:T(8,128)} %bitcast.10), channel_id=1, replica_groups=mesh['zl'=4,'yh'=2,'yl'=2,'x'=4,'core'=2,'zh'=4] {'yl','x','core'}, dimensions={0} | all-to-all | bytes 131072 | tf_op jit(solution)/shard_map/all_to_all | solution.py:351
  28.8 0.0 collective-permute-done.1.got3
  28.8 23.5 %all_to_all.16 = f32[32,8,128]{2,1,0:T(8,128)S(1)} all-to-all(f32[32,8,128]{2,1,0:T(8,128)S(1)} %shard_map.74), channel_id=1, replica_groups=mesh['zl'=4,'yh'=2,'yl'=2,'x'=4,'core'=2,'zh'=4] {'yh','zl','zh'}, dimensions={0} | all-to-all | bytes 262144 | tf_op jit(solution)/shard_map/all_to_all | solution.py:356
  52.3 0.0 copy-done.1
  52.3 6.5 %collective-permute-start.2 = (f32[32,4096]{1,0:T(8,128)S(1)}, f32[32,4096]{1,0:T(8,128)S(1)}, u32[]{:S(2)}, u32[]{:S(2)}) collective-permute-start(f32[32,4096]{1,0:T(8,128)S(1)} %copy-done.1), channel_id=1, source_target_pairs={{0,1},{1,0},{2,3},{3,2},{4,7},{7,4},{5,6},{6,5},{8,9},{9,8},{10,11... | collective-permute-start | bytes 1572872 | tf_op jit(solution)/shard_map/ppermute | solution.py:358
  58.8 0.0 copy-start
  58.8 24.9 %conditional.1 = (f32[128,128]{1,0:T(8,128)S(1)}) conditional(s32[]{:T(128)} %convert_element_type.3, () %tuple.14, (f32[32,8,128]{2,1,0:T(8,128)S(1)}, s32[6]{0:T(128)S(1)}) %tuple.18), branch_computations={%region_0.1_spmd, %region_1.2_spmd} | conditional | bytes 3538992 | solution.py:382
  58.8 0.1 branch_1_fun.2
  58.9 10.7 %all_to_all.14 = f32[8,144,128]{2,1,0:T(8,128)S(1)} all-to-all(f32[8,144,128]{2,1,0:T(8,128)S(1)} %branch_1_fun.2), channel_id=1, replica_groups=mesh['zl'=4,'yh'=2,'yl'=2,'x'=4,'core'=2,'zh'=4] {'yl','x'}, dimensions={0} | all-to-all | bytes 1179648 | tf_op jit(solution)/shard_map/cond/branch_1_fun/all_to_all | solution.py:362
  69.6 6.4 %collective-permute-start = (f32[1152,128]{1,0:T(8,128)S(1)}, f32[1152,128]{1,0:T(8,128)S(1)}, u32[]{:S(2)}, u32[]{:S(2)}) collective-permute-start(f32[1152,128]{1,0:T(8,128)S(1)} %bitcast.8), channel_id=1, source_target_pairs={{0,4},{4,0},{1,5},{5,1},{2,6},{6,2},{3,7},{7,3},{8,12},{12,8},{9,1... | collective-permute-start | bytes 1769480 | tf_op jit(solution)/shard_map/cond/branch_1_fun/ppermute | solution.py:363
  76.0 1.6 %collective-permute-done.other = f32[1152,128]{1,0:T(8,128)S(1)} collective-permute-done((f32[1152,128]{1,0:T(8,128)S(1)}, f32[1152,128]{1,0:T(8,128)S(1)}, u32[]{:S(2)}, u32[]{:S(2)}) %collective-permute-start) | collective-permute-done | bytes 589856 | tf_op jit(solution)/shard_map/cond/branch_1_fun/ppermute | solution.py:363
  77.6 6.2 %branch_1_fun.3 = f32[128,128]{1,0:T(8,128)S(1)} custom-call(s32[6]{0:T(128)S(1)} %get-tuple-element.12.place, f32[1152,128]{1,0:T(8,128)S(1)} %bitcast.9, f32[1152,128]{1,0:T(8,128)S(1)} %collective-permute-done.other), custom_call_target="tpu_custom_call" | custom-call | tf_op jit(solution)/shard_map/cond/branch_1_fun/pallas_call | solution.py:319
  83.8 0.0 collective-permute-done.2.got
  83.8 0.0 copy-done
  83.8 0.4 shard_map.76
  84.1 4.7 %collective-permute-start.3 = (f32[16,4096]{1,0:T(8,128)S(1)}, f32[16,4096]{1,0:T(8,128)S(1)}, u32[]{:S(2)}, u32[]{:S(2)}) collective-permute-start(f32[16,4096]{1,0:T(8,128)S(1)} %shard_map.76), channel_id=1, source_target_pairs={{0,3},{3,0},{1,2},{2,1},{4,5},{5,4},{6,7},{7,6},{8,11},{11,8},{9,1... | collective-permute-start | bytes 786440 | tf_op jit(solution)/shard_map/ppermute | solution.py:384
  88.9 0.0 copy-done.2
  88.9 0.4 shard_map.75
  89.2 13.8 %collective-permute-done.3 = f32[16,4096]{1,0:T(8,128)S(1)} collective-permute-done((f32[16,4096]{1,0:T(8,128)S(1)}, f32[16,4096]{1,0:T(8,128)S(1)}, u32[]{:S(2)}, u32[]{:S(2)}) %collective-permute-start.3) | collective-permute-done | bytes 262176 | tf_op jit(solution)/shard_map/ppermute | solution.py:384
  103.1 0.7 add.3
  (2 shorter events, 0.0 us)
Async XLA Ops:
  0.0 28.8 %collective-permute-start.1 = (f32[16,4096]{1,0:T(8,128)}, f32[16,4096]{1,0:T(8,128)S(1)}, u32[]{:S(2)}, u32[]{:S(2)}) collective-permute-start(f32[16,4096]{1,0:T(8,128)} %own3.3), channel_id=1, source_target_pairs={{0,1},{1,0},{2,3},{3,2},{4,7},{7,4},{5,6},{6,5},{8,9},{9,8},{10,11... | collective-permute-start | bytes 786440 | tf_op jit(solution)/shard_map/ppermute | solution.py:347
  17.4 34.9 %copy-start.1 = (f32[32,4096]{1,0:T(8,128)S(1)}, f32[32,4096]{1,0:T(8,128)}, u32[]{:S(2)}) copy-start(f32[32,4096]{1,0:T(8,128)} %get-tuple-element.28.own) | copy-start | bytes 1572868
  52.3 31.5 %collective-permute-start.2 = (f32[32,4096]{1,0:T(8,128)S(1)}, f32[32,4096]{1,0:T(8,128)S(1)}, u32[]{:S(2)}, u32[]{:S(2)}) collective-permute-start(f32[32,4096]{1,0:T(8,128)S(1)} %copy-done.1), channel_id=1, source_target_pairs={{0,1},{1,0},{2,3},{3,2},{4,7},{7,4},{5,6},{6,5},{8,9},{9,8},{10,11... | collective-permute-start | bytes 1572872 | tf_op jit(solution)/shard_map/ppermute | solution.py:358
  58.8 25.0 %copy-start = (f32[16,4096]{1,0:T(8,128)S(1)}, f32[16,4096]{1,0:T(8,128)}, u32[]{:S(2)}) copy-start(f32[16,4096]{1,0:T(8,128)} %own3.3) | copy-start | bytes 786436
  69.6 8.0 %collective-permute-start = (f32[1152,128]{1,0:T(8,128)S(1)}, f32[1152,128]{1,0:T(8,128)S(1)}, u32[]{:S(2)}, u32[]{:S(2)}) collective-permute-start(f32[1152,128]{1,0:T(8,128)S(1)} %bitcast.8), channel_id=1, source_target_pairs={{0,4},{4,0},{1,5},{5,1},{2,6},{6,2},{3,7},{7,3},{8,12},{12,8},{9,1... | collective-permute-start | bytes 1769480 | tf_op jit(solution)/shard_map/cond/branch_1_fun/ppermute | solution.py:363
  83.7 5.1 %copy-start.2 = (f32[16,4096]{1,0:T(8,128)S(1)}, f32[16,4096]{1,0:T(8,128)}, u32[]{:S(2)}) copy-start(f32[16,4096]{1,0:T(8,128)} %solves.3) | copy-start | bytes 786436
  84.1 18.9 %collective-permute-start.3 = (f32[16,4096]{1,0:T(8,128)S(1)}, f32[16,4096]{1,0:T(8,128)S(1)}, u32[]{:S(2)}, u32[]{:S(2)}) collective-permute-start(f32[16,4096]{1,0:T(8,128)S(1)} %shard_map.76), channel_id=1, source_target_pairs={{0,3},{3,0},{1,2},{2,1},{4,5},{5,4},{6,7},{7,6},{8,11},{11,8},{9,1... | collective-permute-start | bytes 786440 | tf_op jit(solution)/shard_map/ppermute | solution.py:384

commit v6 on v5

--- a/solution.py
+++ b/solution.py
@@ -60,60 +60,75 @@
 
 
 def products(
-    solves, factor3, factor2, factor1, basis3, basis2, basis1, out, own, total3, total21
+    solves, factor3, factor2, factor1, basis3, basis2, basis1, out, own, stacked, bases, sems, done
 ):
-    step = pl.program_id(0)
     dims = (((1,), (1,)), ((), ()))
-    factors = jnp.concatenate([factor2[...], factor1[...]], 0)
-    own[...] = factors
-    high, low = split(jnp.concatenate([solves[...], factor3[...], factors], 0))
-    both = jnp.concatenate([high, low], 0)
-
-    @pl.when(step == 0)
-    def _():
-        total3[...] = jnp.zeros_like(total3)
-        total21[...] = jnp.zeros_like(total21)
-
-    for total, basis in (
-        (total3, basis3[...]),
-        (total21, jnp.concatenate([basis2[...], basis1[...]], 0)),
-    ):
-        top, rest = split(basis)
-        wide = lax.dot_general(both, top, dims, preferred_element_type=f32)
-        thin = lax.dot_general(high, rest, dims, preferred_element_type=f32)
-        total[...] += wide[:RANK] + (wide[RANK:] + thin)
-
-    @pl.when(step == pl.num_programs(0) - 1)
-    def _():
-        deep = total3[...]
-        pieces = [
-            jnp.concatenate([deep[0:16], deep[32:48]], 1),
-            jnp.concatenate([deep[16:32], deep[48:64]], 1),
-            total21[16:32, :],
-            total21[0:16, :],
-            total21[32:48, :],
-            total21[48:64, :],
-            jnp.zeros((16, 128), f32),
-            jnp.zeros((16, 128), f32),
-        ]
-        for index, piece in enumerate(pieces):
-            out[:, 0, index, :] = piece[:8]
-            out[:, 1, index, :] = piece[8:]
+    sources = (solves, factor3, factor2, factor1, basis3, basis2, basis1)
+    starts = (0, 16, 32, 48, 0, 64, 128)
+    copies = []
+    for chunk in range(ROWS // CHUNK):
+        columns = pl.ds(chunk * CHUNK, CHUNK)
+        row = []
+        for index, (source, start) in enumerate(zip(sources, starts)):
+            target = stacked if index < 4 else bases
+            rows = pl.ds(start, source.shape[0])
+            row.append(
+                pltpu.make_async_copy(
+                    source.at[:, columns], target.at[rows, columns], sems.at[chunk, index]
+                )
+            )
+        copies.append(row)
+    for row in copies:
+        for copy in row:
+            copy.start()
+    leaving = pltpu.make_async_copy(stacked.at[pl.ds(2 * LOCAL, 2 * LOCAL), :], own, done)
+    deep = jnp.zeros((RANK, RANK), f32)
+    wide = jnp.zeros((RANK, 2 * RANK), f32)
+    for chunk, row in enumerate(copies):
+        for copy in row:
+            copy.wait()
+        if chunk == ROWS // CHUNK - 1:
+            leaving.start()
+        columns = slice(chunk * CHUNK, (chunk + 1) * CHUNK)
+        high, low = split(stacked[:, columns])
+        both = jnp.concatenate([high, low], 0)
+        sums = []
+        for basis in (bases[:RANK, columns], bases[RANK:, columns]):
+            top, rest = split(basis)
+            main = lax.dot_general(both, top, dims, preferred_element_type=f32)
+            thin = lax.dot_general(high, rest, dims, preferred_element_type=f32)
+            sums.append(main[:RANK] + (main[RANK:] + thin))
+        deep = deep + sums[0]
+        wide = wide + sums[1]
+    pieces = [
+        jnp.concatenate([deep[0:16], deep[32:48]], 1),
+        jnp.concatenate([deep[16:32], deep[48:64]], 1),
+        wide[16:32, :],
+        wide[0:16, :],
+        wide[32:48, :],
+        wide[48:64, :],
+        jnp.zeros((16, 128), f32),
+        jnp.zeros((16, 128), f32),
+    ]
+    for index, piece in enumerate(pieces):
+        out[:, 0, index, :] = piece[:8]
+        out[:, 1, index, :] = piece[8:]
+    leaving.wait()
 
 
 def local_products(*arrays):
-    narrow = pl.BlockSpec((LOCAL, CHUNK), lambda i: (0, i))
-    wide = pl.BlockSpec((RANK, CHUNK), lambda i: (0, i))
+    anywhere = pl.BlockSpec(memory_space=pl.ANY)
     return pl.pallas_call(
         products,
-        grid=(ROWS // CHUNK,),
-        in_specs=[narrow] * 4 + [wide] * 3,
-        out_specs=(
-            pl.BlockSpec((8, 2, 8, 128), lambda i: (0, 0, 0, 0)),
-            pl.BlockSpec((2 * LOCAL, CHUNK), lambda i: (0, i)),
-        ),
+        in_specs=[anywhere] * 7,
+        out_specs=(pl.BlockSpec(memory_space=pltpu.VMEM), anywhere),
         out_shape=(shape(8, 2, 8, 128), shape(2 * LOCAL, ROWS)),
-        scratch_shapes=[pltpu.VMEM((RANK, RANK), f32), pltpu.VMEM((RANK, 2 * RANK), f32)],
+        scratch_shapes=[
+            pltpu.VMEM((RANK, ROWS), f32),
+            pltpu.VMEM((3 * RANK, ROWS), f32),
+            pltpu.SemaphoreType.DMA((ROWS // CHUNK, 7)),
+            pltpu.SemaphoreType.DMA,
+        ],
         cost_estimate=FREE,
     )(*arrays)
 

time: 105 us -> 105 us (level)
  no operation moved by 1% of the time
where the time goes in v6:
time: 105 us; the launch traced here: 104 us
  blocking collectives  45.6 us (43%)
  starting transfers between devices  30.9 us (29%)
  waiting for transfers between devices  15.5 us (15%)
  Pallas kernels  10.9 us (10%)
    all_to_all x1, blocking collectives, on_device(): slabs = lax.all_to_all(copies, SLAB, 0, 0, tiled=True)  23.5 us
    ppermute x1, waiting for transfers between devices, on_device(): came = lax.ppermute(sent, PAIRS, RETURN)  13.9 us
    ppermute x1, starting transfers between devices, on_device(): got3 = lax.ppermute(factor3, PAIRS, SWAP)  13.3 us
    all_to_all x1, blocking collectives, on_device(): pieces = lax.all_to_all(slots, LEAF, 0, 0, tiled=True)  11.4 us
    all_to_all x1, blocking collectives, solve(): lax.all_to_all(message, ('yl', 'x'), 0, 0, tiled=True)  10.7 us
    pallas_call x5, Pallas kernels, call(): pl.pallas_call(kernel, out_shape=shapes, scratch_shapes=list(scratch), co...  7 us
    ppermute x1, starting transfers between devices, solve(): other = lax.ppermute(mine, 'core', [(0, 1), (1, 0)])  6.61 us
    ppermute x1, starting transfers between devices, on_device(): got = lax.ppermute(own, PAIRS, SWAP)  6.33 us
  transfers between devices with their start and end apart: 4, of which 2 were waited for; matrix products, arithmetic and copies ran while one was open for 0% of the time, Pallas kernels for 10%

profile of v6, /device:TPU:1, one launch (start us, length us, event | category | flops | bytes accessed | tf_op | source)
XLA Modules:
  0.0 103.8 jit_solution(9821908516425081331)
XLA Ops:
  0.0 13.3 %collective-permute-start.1 = (f32[16,4096]{1,0:T(8,128)}, f32[16,4096]{1,0:T(8,128)S(1)}, u32[]{:S(2)}, u32[]{:S(2)}) collective-permute-start(f32[16,4096]{1,0:T(8,128)} %own3.3), channel_id=1, source_target_pairs={{0,1},{1,0},{2,3},{3,2},{4,7},{7,4},{5,6},{6,5},{8,9},{9,8},{10,11... | collective-permute-start | bytes 786440 | tf_op jit(solution)/shard_map/ppermute | solution.py:362
  13.3 0.1 stack.27
  13.4 3.9 %shard_map.73 = (f32[8,2,8,128]{3,2,1,0:T(8,128)}, f32[32,4096]{1,0:T(8,128)}) custom-call(f32[16,4096]{1,0:T(8,128)} %solves.3, f32[16,4096]{1,0:T(8,128)} %own3.3, f32[16,4096]{1,0:T(8,128)} %factor2.1, f32[16,4096]{1,0:T(8,128)} %factor1.1, f32[64,4096]{1,0:T(8,128)} %basis3.1, f32[64,4096]{1,0:T(8,128)} %basis2.1, f32[64,4096]{1,0:T(8,128)} %basis1.1), custom_call_target="tpu_custom_call" | custom-call | tf_op jit(solution)/shard_map/pallas_call | solution.py:121
  17.3 0.0 copy-start.1
  17.3 11.4 %all_to_all.15.pieces = f32[16,8,128]{2,1,0:T(8,128)S(1)} all-to-all(f32[16,8,128]{2,1,0:T(8,128)} %bitcast.10), channel_id=1, replica_groups=mesh['zl'=4,'yh'=2,'yl'=2,'x'=4,'core'=2,'zh'=4] {'yl','x','core'}, dimensions={0} | all-to-all | bytes 131072 | tf_op jit(solution)/shard_map/all_to_all | solution.py:366
  28.7 0.0 collective-permute-done.1.got3
  28.7 23.5 %all_to_all.16 = f32[32,8,128]{2,1,0:T(8,128)S(1)} all-to-all(f32[32,8,128]{2,1,0:T(8,128)S(1)} %shard_map.74), channel_id=1, replica_groups=mesh['zl'=4,'yh'=2,'yl'=2,'x'=4,'core'=2,'zh'=4] {'yh','zl','zh'}, dimensions={0} | all-to-all | bytes 262144 | tf_op jit(solution)/shard_map/all_to_all | solution.py:371
  52.2 0.0 copy-done.1
  52.2 6.3 %collective-permute-start.2 = (f32[32,4096]{1,0:T(8,128)S(1)}, f32[32,4096]{1,0:T(8,128)S(1)}, u32[]{:S(2)}, u32[]{:S(2)}) collective-permute-start(f32[32,4096]{1,0:T(8,128)S(1)} %copy-done.1), channel_id=1, source_target_pairs={{0,1},{1,0},{2,3},{3,2},{4,7},{7,4},{5,6},{6,5},{8,9},{9,8},{10,11... | collective-permute-start | bytes 1572872 | tf_op jit(solution)/shard_map/ppermute | solution.py:373
  58.6 0.0 copy-start
  58.6 25.2 %conditional.1 = (f32[128,128]{1,0:T(8,128)S(1)}) conditional(s32[]{:T(128)} %convert_element_type.3, () %tuple.14, (f32[32,8,128]{2,1,0:T(8,128)S(1)}, s32[6]{0:T(128)S(1)}) %tuple.18), branch_computations={%region_0.1_spmd, %region_1.2_spmd} | conditional | bytes 3538992 | solution.py:397
  58.6 0.1 branch_1_fun.2
  58.7 10.7 %all_to_all.14 = f32[8,144,128]{2,1,0:T(8,128)S(1)} all-to-all(f32[8,144,128]{2,1,0:T(8,128)S(1)} %branch_1_fun.2), channel_id=1, replica_groups=mesh['zl'=4,'yh'=2,'yl'=2,'x'=4,'core'=2,'zh'=4] {'yl','x'}, dimensions={0} | all-to-all | bytes 1179648 | tf_op jit(solution)/shard_map/cond/branch_1_fun/all_to_all | solution.py:377
  69.3 6.6 %collective-permute-start = (f32[1152,128]{1,0:T(8,128)S(1)}, f32[1152,128]{1,0:T(8,128)S(1)}, u32[]{:S(2)}, u32[]{:S(2)}) collective-permute-start(f32[1152,128]{1,0:T(8,128)S(1)} %bitcast.8), channel_id=1, source_target_pairs={{0,4},{4,0},{1,5},{5,1},{2,6},{6,2},{3,7},{7,3},{8,12},{12,8},{9,1... | collective-permute-start | bytes 1769480 | tf_op jit(solution)/shard_map/cond/branch_1_fun/ppermute | solution.py:378
  76.0 1.6 %collective-permute-done.other = f32[1152,128]{1,0:T(8,128)S(1)} collective-permute-done((f32[1152,128]{1,0:T(8,128)S(1)}, f32[1152,128]{1,0:T(8,128)S(1)}, u32[]{:S(2)}, u32[]{:S(2)}) %collective-permute-start) | collective-permute-done | bytes 589856 | tf_op jit(solution)/shard_map/cond/branch_1_fun/ppermute | solution.py:378
  77.6 6.2 %branch_1_fun.3 = f32[128,128]{1,0:T(8,128)S(1)} custom-call(s32[6]{0:T(128)S(1)} %get-tuple-element.12.place, f32[1152,128]{1,0:T(8,128)S(1)} %bitcast.9, f32[1152,128]{1,0:T(8,128)S(1)} %collective-permute-done.other), custom_call_target="tpu_custom_call" | custom-call | tf_op jit(solution)/shard_map/cond/branch_1_fun/pallas_call | solution.py:334
  83.8 0.0 collective-permute-done.2.got
  83.8 0.0 copy-done
  83.8 0.4 shard_map.76
  84.1 4.7 %collective-permute-start.3 = (f32[16,4096]{1,0:T(8,128)S(1)}, f32[16,4096]{1,0:T(8,128)S(1)}, u32[]{:S(2)}, u32[]{:S(2)}) collective-permute-start(f32[16,4096]{1,0:T(8,128)S(1)} %shard_map.76), channel_id=1, source_target_pairs={{0,3},{3,0},{1,2},{2,1},{4,5},{5,4},{6,7},{7,6},{8,11},{11,8},{9,1... | collective-permute-start | bytes 786440 | tf_op jit(solution)/shard_map/ppermute | solution.py:399
  88.9 0.0 copy-done.2
  88.9 0.4 shard_map.75
  89.2 13.9 %collective-permute-done.3 = f32[16,4096]{1,0:T(8,128)S(1)} collective-permute-done((f32[16,4096]{1,0:T(8,128)S(1)}, f32[16,4096]{1,0:T(8,128)S(1)}, u32[]{:S(2)}, u32[]{:S(2)}) %collective-permute-start.3) | collective-permute-done | bytes 262176 | tf_op jit(solution)/shard_map/ppermute | solution.py:399
  103.1 0.7 add.3
  (2 shorter events, 0.0 us)
Async XLA Ops:
  0.0 28.7 %collective-permute-start.1 = (f32[16,4096]{1,0:T(8,128)}, f32[16,4096]{1,0:T(8,128)S(1)}, u32[]{:S(2)}, u32[]{:S(2)}) collective-permute-start(f32[16,4096]{1,0:T(8,128)} %own3.3), channel_id=1, source_target_pairs={{0,1},{1,0},{2,3},{3,2},{4,7},{7,4},{5,6},{6,5},{8,9},{9,8},{10,11... | collective-permute-start | bytes 786440 | tf_op jit(solution)/shard_map/ppermute | solution.py:362
  17.3 34.9 %copy-start.1 = (f32[32,4096]{1,0:T(8,128)S(1)}, f32[32,4096]{1,0:T(8,128)}, u32[]{:S(2)}) copy-start(f32[32,4096]{1,0:T(8,128)} %get-tuple-element.28.own) | copy-start | bytes 1572868
  52.2 31.5 %collective-permute-start.2 = (f32[32,4096]{1,0:T(8,128)S(1)}, f32[32,4096]{1,0:T(8,128)S(1)}, u32[]{:S(2)}, u32[]{:S(2)}) collective-permute-start(f32[32,4096]{1,0:T(8,128)S(1)} %copy-done.1), channel_id=1, source_target_pairs={{0,1},{1,0},{2,3},{3,2},{4,7},{7,4},{5,6},{6,5},{8,9},{9,8},{10,11... | collective-permute-start | bytes 1572872 | tf_op jit(solution)/shard_map/ppermute | solution.py:373
  58.6 25.2 %copy-start = (f32[16,4096]{1,0:T(8,128)S(1)}, f32[16,4096]{1,0:T(8,128)}, u32[]{:S(2)}) copy-start(f32[16,4096]{1,0:T(8,128)} %own3.3) | copy-start | bytes 786436
  69.3 8.2 %collective-permute-start = (f32[1152,128]{1,0:T(8,128)S(1)}, f32[1152,128]{1,0:T(8,128)S(1)}, u32[]{:S(2)}, u32[]{:S(2)}) collective-permute-start(f32[1152,128]{1,0:T(8,128)S(1)} %bitcast.8), channel_id=1, source_target_pairs={{0,4},{4,0},{1,5},{5,1},{2,6},{6,2},{3,7},{7,3},{8,12},{12,8},{9,1... | collective-permute-start | bytes 1769480 | tf_op jit(solution)/shard_map/cond/branch_1_fun/ppermute | solution.py:378
  83.7 5.1 %copy-start.2 = (f32[16,4096]{1,0:T(8,128)S(1)}, f32[16,4096]{1,0:T(8,128)}, u32[]{:S(2)}) copy-start(f32[16,4096]{1,0:T(8,128)} %solves.3) | copy-start | bytes 786436
  84.1 19.0 %collective-permute-start.3 = (f32[16,4096]{1,0:T(8,128)S(1)}, f32[16,4096]{1,0:T(8,128)S(1)}, u32[]{:S(2)}, u32[]{:S(2)}) collective-permute-start(f32[16,4096]{1,0:T(8,128)S(1)} %shard_map.76), channel_id=1, source_target_pairs={{0,3},{3,0},{1,2},{2,1},{4,5},{5,4},{6,7},{7,6},{8,11},{11,8},{9,1... | collective-permute-start | bytes 786440 | tf_op jit(solution)/shard_map/ppermute | solution.py:399

commit v7 on v5

--- a/solution.py
+++ b/solution.py
@@ -200,13 +200,24 @@
 
 def merge(nodes, scratch, couples=()):
     crossed = [full(kb, ka) for ka, kb, _, _ in nodes]
-    sides = [ra - exact(rb, ka) for ka, _, ra, rb in nodes]
-    known = [exact(node[3], ca) for node, (ca, _) in zip(nodes, couples)]
+    after = [c.shape[1] for c, _ in couples] or [0] * len(nodes)
+    firsts = [[c] for c, _ in couples] or [[] for _ in nodes]
+    shared = [
+        exact(rb, jnp.concatenate(first + [ka], 1))
+        for (ka, _, _, rb), first in zip(nodes, firsts)
+    ]
+    sides = [node[2] - both[:, at:] for node, both, at in zip(nodes, shared, after)]
+    known = [both[:, :at] for both, at in zip(shared, after)]
     gains = [cb - exact(node[1], ca) for node, (ca, cb) in zip(nodes, couples)]
     inverses(crossed, scratch)
     bottoms = [exact(side, scratch[index]) for index, side in enumerate(sides)]
-    tops = [rb - exact(low, kb) for (_, kb, _, rb), low in zip(nodes, bottoms)]
-    updates = [first + exact(low, gain) for first, low, gain in zip(known, bottoms, gains)]
+    seconds = [[gain] for gain in gains] or [[] for _ in nodes]
+    applied = [
+        exact(low, jnp.concatenate(second + [node[1]], 1))
+        for low, second, node in zip(bottoms, seconds, nodes)
+    ]
+    tops = [node[3] - both[:, at:] for node, both, at in zip(nodes, applied, after)]
+    updates = [first + both[:, :at] for first, both, at in zip(known, applied, after) if at]
     return tops, bottoms, updates
 
 

time: 105 us -> 105 us (level)
  no operation moved by 1% of the time
where the time goes in v7:
time: 105 us; the launch traced here: 104 us
  blocking collectives  45.6 us (43%)
  starting transfers between devices  30.8 us (29%)
  waiting for transfers between devices  15.5 us (15%)
  Pallas kernels  10.9 us (10%)
    all_to_all x1, blocking collectives, on_device(): slabs = lax.all_to_all(copies, SLAB, 0, 0, tiled=True)  23.5 us
    ppermute x1, waiting for transfers between devices, on_device(): came = lax.ppermute(sent, PAIRS, RETURN)  13.8 us
    ppermute x1, starting transfers between devices, on_device(): got3 = lax.ppermute(factor3, PAIRS, SWAP)  13.3 us
    all_to_all x1, blocking collectives, on_device(): pieces = lax.all_to_all(slots, LEAF, 0, 0, tiled=True)  11.4 us
    all_to_all x1, blocking collectives, solve(): lax.all_to_all(message, ('yl', 'x'), 0, 0, tiled=True)  10.7 us
    pallas_call x5, Pallas kernels, call(): pl.pallas_call(kernel, out_shape=shapes, scratch_shapes=list(scratch), co...  6.94 us
    ppermute x1, starting transfers between devices, on_device(): got = lax.ppermute(own, PAIRS, SWAP)  6.49 us
    ppermute x1, starting transfers between devices, solve(): other = lax.ppermute(mine, 'core', [(0, 1), (1, 0)])  6.37 us
  transfers between devices with their start and end apart: 4, of which 2 were waited for; matrix products, arithmetic and copies ran while one was open for 0% of the time, Pallas kernels for 10%

profile of v7, /device:TPU:1, one launch (start us, length us, event | category | flops | bytes accessed | tf_op | source)
XLA Modules:
  0.0 103.7 jit_solution(12236896642405878212)
XLA Ops:
  0.0 13.3 %collective-permute-start.1 = (f32[16,4096]{1,0:T(8,128)}, f32[16,4096]{1,0:T(8,128)S(1)}, u32[]{:S(2)}, u32[]{:S(2)}) collective-permute-start(f32[16,4096]{1,0:T(8,128)} %own3.3), channel_id=1, source_target_pairs={{0,1},{1,0},{2,3},{3,2},{4,7},{7,4},{5,6},{6,5},{8,9},{9,8},{10,11... | collective-permute-start | bytes 786440 | tf_op jit(solution)/shard_map/ppermute | solution.py:358
  13.3 0.1 stack.27
  13.4 4.0 %shard_map.73 = (f32[8,2,8,128]{3,2,1,0:T(8,128)}, f32[32,4096]{1,0:T(8,128)}) custom-call(f32[16,4096]{1,0:T(8,128)} %solves.3, f32[16,4096]{1,0:T(8,128)} %own3.3, f32[16,4096]{1,0:T(8,128)} %factor2.1, f32[16,4096]{1,0:T(8,128)} %factor1.1, f32[64,4096]{1,0:T(8,128)} %basis3.1, f32[64,4096]{1,0:T(8,128)} %basis2.1, f32[64,4096]{1,0:T(8,128)} %basis1.1), custom_call_target="tpu_custom_call" | custom-call | tf_op jit(solution)/shard_map/pallas_call | solution.py:107
  17.4 0.0 copy-start.1
  17.4 11.4 %all_to_all.15.pieces = f32[16,8,128]{2,1,0:T(8,128)S(1)} all-to-all(f32[16,8,128]{2,1,0:T(8,128)} %bitcast.10), channel_id=1, replica_groups=mesh['zl'=4,'yh'=2,'yl'=2,'x'=4,'core'=2,'zh'=4] {'yl','x','core'}, dimensions={0} | all-to-all | bytes 131072 | tf_op jit(solution)/shard_map/all_to_all | solution.py:362
  28.8 0.0 collective-permute-done.1.got3
  28.8 23.5 %all_to_all.16 = f32[32,8,128]{2,1,0:T(8,128)S(1)} all-to-all(f32[32,8,128]{2,1,0:T(8,128)S(1)} %shard_map.74), channel_id=1, replica_groups=mesh['zl'=4,'yh'=2,'yl'=2,'x'=4,'core'=2,'zh'=4] {'yh','zl','zh'}, dimensions={0} | all-to-all | bytes 262144 | tf_op jit(solution)/shard_map/all_to_all | solution.py:367
  52.3 0.0 copy-done.1
  52.3 6.5 %collective-permute-start.2 = (f32[32,4096]{1,0:T(8,128)S(1)}, f32[32,4096]{1,0:T(8,128)S(1)}, u32[]{:S(2)}, u32[]{:S(2)}) collective-permute-start(f32[32,4096]{1,0:T(8,128)S(1)} %copy-done.1), channel_id=1, source_target_pairs={{0,1},{1,0},{2,3},{3,2},{4,7},{7,4},{5,6},{6,5},{8,9},{9,8},{10,11... | collective-permute-start | bytes 1572872 | tf_op jit(solution)/shard_map/ppermute | solution.py:369
  58.8 0.0 copy-start
  58.8 24.9 %conditional.1 = (f32[128,128]{1,0:T(8,128)S(1)}) conditional(s32[]{:T(128)} %convert_element_type.3, () %tuple.14, (f32[32,8,128]{2,1,0:T(8,128)S(1)}, s32[6]{0:T(128)S(1)}) %tuple.18), branch_computations={%region_0.1_spmd, %region_1.2_spmd} | conditional | bytes 3538992 | solution.py:393
  58.8 0.1 branch_1_fun.2
  58.9 10.7 %all_to_all.14 = f32[8,144,128]{2,1,0:T(8,128)S(1)} all-to-all(f32[8,144,128]{2,1,0:T(8,128)S(1)} %branch_1_fun.2), channel_id=1, replica_groups=mesh['zl'=4,'yh'=2,'yl'=2,'x'=4,'core'=2,'zh'=4] {'yl','x'}, dimensions={0} | all-to-all | bytes 1179648 | tf_op jit(solution)/shard_map/cond/branch_1_fun/all_to_all | solution.py:373
  69.6 6.4 %collective-permute-start = (f32[1152,128]{1,0:T(8,128)S(1)}, f32[1152,128]{1,0:T(8,128)S(1)}, u32[]{:S(2)}, u32[]{:S(2)}) collective-permute-start(f32[1152,128]{1,0:T(8,128)S(1)} %bitcast.8), channel_id=1, source_target_pairs={{0,4},{4,0},{1,5},{5,1},{2,6},{6,2},{3,7},{7,3},{8,12},{12,8},{9,1... | collective-permute-start | bytes 1769480 | tf_op jit(solution)/shard_map/cond/branch_1_fun/ppermute | solution.py:374
  76.0 1.6 %collective-permute-done.other = f32[1152,128]{1,0:T(8,128)S(1)} collective-permute-done((f32[1152,128]{1,0:T(8,128)S(1)}, f32[1152,128]{1,0:T(8,128)S(1)}, u32[]{:S(2)}, u32[]{:S(2)}) %collective-permute-start) | collective-permute-done | bytes 589856 | tf_op jit(solution)/shard_map/cond/branch_1_fun/ppermute | solution.py:374
  77.6 6.1 %branch_1_fun.3 = f32[128,128]{1,0:T(8,128)S(1)} custom-call(s32[6]{0:T(128)S(1)} %get-tuple-element.12.place, f32[1152,128]{1,0:T(8,128)S(1)} %bitcast.9, f32[1152,128]{1,0:T(8,128)S(1)} %collective-permute-done.other), custom_call_target="tpu_custom_call" | custom-call | tf_op jit(solution)/shard_map/cond/branch_1_fun/pallas_call | solution.py:330
  83.7 0.0 collective-permute-done.2.got
  83.7 0.0 copy-done
  83.7 0.4 shard_map.76
  84.1 4.7 %collective-permute-start.3 = (f32[16,4096]{1,0:T(8,128)S(1)}, f32[16,4096]{1,0:T(8,128)S(1)}, u32[]{:S(2)}, u32[]{:S(2)}) collective-permute-start(f32[16,4096]{1,0:T(8,128)S(1)} %shard_map.76), channel_id=1, source_target_pairs={{0,3},{3,0},{1,2},{2,1},{4,5},{5,4},{6,7},{7,6},{8,11},{11,8},{9,1... | collective-permute-start | bytes 786440 | tf_op jit(solution)/shard_map/ppermute | solution.py:395
  88.8 0.0 copy-done.2
  88.8 0.4 shard_map.75
  89.2 13.8 %collective-permute-done.3 = f32[16,4096]{1,0:T(8,128)S(1)} collective-permute-done((f32[16,4096]{1,0:T(8,128)S(1)}, f32[16,4096]{1,0:T(8,128)S(1)}, u32[]{:S(2)}, u32[]{:S(2)}) %collective-permute-start.3) | collective-permute-done | bytes 262176 | tf_op jit(solution)/shard_map/ppermute | solution.py:395
  103.0 0.7 add.3
  (2 shorter events, 0.0 us)
Async XLA Ops:
  0.0 28.8 %collective-permute-start.1 = (f32[16,4096]{1,0:T(8,128)}, f32[16,4096]{1,0:T(8,128)S(1)}, u32[]{:S(2)}, u32[]{:S(2)}) collective-permute-start(f32[16,4096]{1,0:T(8,128)} %own3.3), channel_id=1, source_target_pairs={{0,1},{1,0},{2,3},{3,2},{4,7},{7,4},{5,6},{6,5},{8,9},{9,8},{10,11... | collective-permute-start | bytes 786440 | tf_op jit(solution)/shard_map/ppermute | solution.py:358
  17.4 34.9 %copy-start.1 = (f32[32,4096]{1,0:T(8,128)S(1)}, f32[32,4096]{1,0:T(8,128)}, u32[]{:S(2)}) copy-start(f32[32,4096]{1,0:T(8,128)} %get-tuple-element.28.own) | copy-start | bytes 1572868
  52.3 31.4 %collective-permute-start.2 = (f32[32,4096]{1,0:T(8,128)S(1)}, f32[32,4096]{1,0:T(8,128)S(1)}, u32[]{:S(2)}, u32[]{:S(2)}) collective-permute-start(f32[32,4096]{1,0:T(8,128)S(1)} %copy-done.1), channel_id=1, source_target_pairs={{0,1},{1,0},{2,3},{3,2},{4,7},{7,4},{5,6},{6,5},{8,9},{9,8},{10,11... | collective-permute-start | bytes 1572872 | tf_op jit(solution)/shard_map/ppermute | solution.py:369
  58.8 24.9 %copy-start = (f32[16,4096]{1,0:T(8,128)S(1)}, f32[16,4096]{1,0:T(8,128)}, u32[]{:S(2)}) copy-start(f32[16,4096]{1,0:T(8,128)} %own3.3) | copy-start | bytes 786436
  69.6 8.0 %collective-permute-start = (f32[1152,128]{1,0:T(8,128)S(1)}, f32[1152,128]{1,0:T(8,128)S(1)}, u32[]{:S(2)}, u32[]{:S(2)}) collective-permute-start(f32[1152,128]{1,0:T(8,128)S(1)} %bitcast.8), channel_id=1, source_target_pairs={{0,4},{4,0},{1,5},{5,1},{2,6},{6,2},{3,7},{7,3},{8,12},{12,8},{9,1... | collective-permute-start | bytes 1769480 | tf_op jit(solution)/shard_map/cond/branch_1_fun/ppermute | solution.py:374
  83.7 5.1 %copy-start.2 = (f32[16,4096]{1,0:T(8,128)S(1)}, f32[16,4096]{1,0:T(8,128)}, u32[]{:S(2)}) copy-start(f32[16,4096]{1,0:T(8,128)} %solves.3) | copy-start | bytes 786436
  84.1 18.9 %collective-permute-start.3 = (f32[16,4096]{1,0:T(8,128)S(1)}, f32[16,4096]{1,0:T(8,128)S(1)}, u32[]{:S(2)}, u32[]{:S(2)}) collective-permute-start(f32[16,4096]{1,0:T(8,128)S(1)} %shard_map.76), channel_id=1, source_target_pairs={{0,3},{3,0},{1,2},{2,1},{4,5},{5,4},{6,7},{7,6},{8,11},{11,8},{9,1... | collective-permute-start | bytes 786440 | tf_op jit(solution)/shard_map/ppermute | solution.py:395
